TPU v7x, 32 devices: a whole 2x2x4 slice. The times are simulated.
32 devices in a mesh: dp: 16 (over z, x, core), fsdp: 2 (over y).
Axes of the slice: x: 2, y: 2, z: 4, core: 2. Of those that a mesh axis runs over, the one named last changes fastest.
Arguments:
- picture_mean_embeddings: bfloat16 [640, 1152], P(('dp', 'fsdp')), may hold values from -0.1875 to 0.1875
- caption_tower_summary: bfloat16 [640, 1152], P(('dp', 'fsdp')), may hold values from -0.125 to 0.125
- caption_mapping_matrix: bfloat16 [1152, 1152], P('fsdp'), may hold values from -0.125 to 1
- picture_match_index: int32 [640], P('dp'), may hold values from 0 to 639, as said below
- sharpness_factor: float32 [1], replicated, may hold values from 40 to 56
- score_shift_term: float32 [1], replicated, may hold values from -11 to -10
Outputs:
- grad_image: float32 [640, 1152], P(('dp', 'fsdp'))
- grad_text: float32 [640, 1152], P(('dp', 'fsdp'))
- head_grad: float32 [1152, 1152], P('fsdp')
Inputs may be any that keep to these rules, and one draw needn't show every extreme that they name: `picture_match_index`: every text is the pair of exactly one image.
All inputs are finite; a program needn't handle non-finite values.
Results may differ from a plain program's by a relative error of at most 0.0086.
Values may be sent and summed in bfloat16 or wider, within the bound.
No kernel may reach another device: no remote copies, remote signals or barrier semaphores. Data moves between devices by JAX's collectives and lax.ppermute only.
A program may use at most 64 MiB of HBM per device.

v0:
```python
import functools

import jax
import jax.numpy as jnp
from jax import lax
from jax.experimental import pallas as pl
from jax.experimental.pallas import tpu as pltpu
from jax.sharding import PartitionSpec as P

epsilon = 1e-06


def passed_along(block, axis, distance):
    devices = range(lax.axis_size(axis))
    route = [((i - distance) % len(devices), i) for i in devices]
    return lax.ppermute(block, axis, route)


def normalize(values):
    norms = jnp.sqrt(jnp.sum(values * values, axis=1, keepdims=True) + epsilon)
    return (values / norms, norms)


def unproject(grad_unit, unit, norms):
    return (grad_unit - unit * jnp.sum(unit * grad_unit, axis=1, keepdims=True)) / norms


def ring_plan(
    picture_mean_embeddings,
    caption_tower_summary,
    caption_mapping_matrix,
    picture_match_index,
    sharpness_factor,
    score_shift_term,
):
    rows = caption_tower_summary.shape[0]
    width = caption_mapping_matrix.shape[1]
    cycle_size = lax.axis_size("dp")
    column_count = lax.axis_size("fsdp")
    cycle_index = lax.axis_index("dp")
    column_index = lax.axis_index("fsdp")
    score_multiplier = sharpness_factor[0]
    offset = score_shift_term[0]
    feature_column_set = lax.all_to_all(
        caption_tower_summary, "fsdp", split_axis=1, concat_axis=0, tiled=True
    )
    projected = jnp.dot(
        caption_tower_summary,
        lax.all_gather(caption_mapping_matrix, "fsdp", axis=0, tiled=True),
        preferred_element_type=jnp.float32,
    )
    unit_text, text_norm = normalize(projected)
    text_unit = unit_text.astype(jnp.bfloat16)
    unit_image, image_norm = normalize(picture_mean_embeddings.astype(jnp.float32))
    image_unit = lax.all_gather(unit_image.astype(jnp.bfloat16), "fsdp", axis=0, tiled=True)
    group = image_unit.shape[0]

    def tile(block, text_rows):
        scores = lax.dot_general(
            image_unit, block, (((1,), (1,)), ((), ())), preferred_element_type=jnp.float32
        )
        logits = score_multiplier * scores + offset
        sign = jnp.where(picture_match_index[:, None] == text_rows[None, :], 1.0, -1.0).astype(
            jnp.float32
        )
        weights = (score_multiplier * -sign * jax.nn.sigmoid(-sign * logits)).astype(jnp.bfloat16)
        image_part = jnp.dot(weights, block, preferred_element_type=jnp.float32)
        text_part = lax.dot_general(
            weights, image_unit, (((0,), (0,)), ((), ())), preferred_element_type=jnp.float32
        )
        return (image_part, text_part)

    def rows_of(owner, count):
        return (owner * column_count + column_index) * rows + jnp.arange(count, dtype=jnp.int32)

    image_start = jnp.zeros((group, width), jnp.float32)

    def advance(count, state):
        block, carried, image_sum = state
        owner = (cycle_index - count) % cycle_size
        image_part, text_part = tile(block, rows_of(owner, rows))
        block = passed_along(block, "dp", 1)
        carried = passed_along(carried + text_part, "dp", 1)
        return (block, carried, image_sum + image_part)

    state = (text_unit, jnp.zeros((rows, width), jnp.float32), image_start)
    block, grad_zt, image_sum = lax.fori_loop(0, cycle_size, advance, state)
    grad_zi = lax.psum_scatter(image_sum, "fsdp", scatter_dimension=0, tiled=True)
    grad_image = unproject(grad_zi, unit_image, image_norm)
    grad_proj = unproject(grad_zt, unit_text, text_norm).astype(jnp.bfloat16)
    grad_group = lax.all_gather(grad_proj, "fsdp", axis=0, tiled=True)
    head_part = lax.dot_general(
        feature_column_set, grad_group, (((0,), (0,)), ((), ())), preferred_element_type=jnp.float32
    )
    head_grad = lax.psum(head_part, "dp")
    grad_text = lax.dot_general(
        grad_proj,
        lax.all_gather(caption_mapping_matrix, "fsdp", axis=0, tiled=True),
        (((1,), (1,)), ((), ())),
        preferred_element_type=jnp.float32,
    )
    return (grad_image, grad_text, head_grad)


def across(block, bits):
    count = lax.axis_size("dp") * lax.axis_size("fsdp")
    return lax.ppermute(block, ("dp", "fsdp"), [(i, i ^ bits) for i in range(count)])


Y, CORE, X, Z1, Z2 = 1, 2, 4, 8, 16
IMAGE_ORDER = (Y, Z2, X, Z1, CORE)
TEXT_ORDER = (Y, Z2, Z1, CORE, X)
NT = (((1,), (1,)), ((), ()))
TN = (((0,), (0,)), ((), ()))


def dot(a, b, dims=(((1,), (0,)), ((), ()))):
    return lax.dot_general(a, b, dims, preferred_element_type=jnp.float32)


def cuts(size, step):
    return [slice(k, min(k + step, size)) for k in range(0, size, step)]


def owners(order, shape, axis, rows, place):
    row = lax.broadcasted_iota(jnp.int32, shape, axis)
    block = sum((row >= k * rows).astype(jnp.int32) for k in range(1, shape[axis] // rows))
    owner = jnp.zeros_like(row)
    for k, bits in enumerate(order):
        owner += ((block >> k) & 1) * bits
    return owner ^ place, row - block * rows


def weigh(scores, paired, scalars):
    sharpness, shift = scalars[:, 0:1], scalars[:, 1:2]
    logits = sharpness * scores + shift
    share = 1.0 / (1.0 + jnp.exp(jnp.where(paired, logits, -logits)))
    return (jnp.where(paired, -sharpness, sharpness) * share).astype(jnp.bfloat16)


def own_kernel(image, text, matrix, match, own, quarter, images, texts, indices, digits, sems):
    rows = images.shape[0]
    count = quarter.shape[0]
    start = pl.multiple_of(lax.rem(lax.axis_index("dp"), 2) * count, 32)
    pairs = ((image, images), (text, texts), (match, indices))
    pairs += ((matrix.at[pl.ds(start, count)], quarter),)
    copies = [pltpu.make_async_copy(*pair, sems.at[k]) for k, pair in enumerate(pairs)]
    for copy in copies:
        copy.start()
    for copy in copies[:3]:
        copy.wait()
    width = indices.shape[1]
    digits[...] = jnp.zeros(digits.shape, jnp.float32)
    digits[0:1, :width] = (indices[...] >> 5).astype(jnp.float32)
    digits[1:2, :width] = (indices[...] & 31).astype(jnp.float32)
    spare = digits[: own.shape[1] - rows]
    unit_image, _ = normalize(images[...].astype(jnp.float32))
    own[0] = jnp.concatenate([unit_image, spare]).astype(jnp.bfloat16)
    text_rows = texts[...].astype(jnp.float32)
    own[1] = jnp.concatenate([text_rows, jnp.zeros_like(spare)]).astype(jnp.bfloat16)
    copies[3].wait()


def pair_indices(rows, total, pieces, side):
    digits = jnp.concatenate([piece[-8:, :128].astype(jnp.float32) for piece in pieces])
    lane = lax.broadcasted_iota(jnp.int32, (1, total), 1)
    group = sum((lane >= k).astype(jnp.int32) for k in range(2 * rows, total, 2 * rows))
    row = lane - group * 2 * rows
    row = jnp.where(side == 0, row, jnp.where(row < rows, row + rows, row - rows))
    chosen = lax.broadcasted_iota(jnp.int32, (128, total), 0) == row
    spread = dot(digits.astype(jnp.bfloat16), chosen.astype(jnp.float32).astype(jnp.bfloat16))
    number = lax.broadcasted_iota(jnp.int32, spread.shape, 0)
    scale = jnp.where(number == 2 * group, 32.0, jnp.where(number == 2 * group + 1, 1.0, 0.0))
    return jnp.sum(scale * spread, axis=0, keepdims=True).astype(jnp.int32)


def project(text, matrix, projected, zt):
    for cut in cuts(matrix.shape[1], 256):
        projected[:, cut] = dot(text[...], matrix[:, cut])
    for block in cuts(text.shape[0], 160):
        value = projected[block]
        inverse = lax.rsqrt(jnp.sum(value * value, axis=1, keepdims=True) + epsilon)
        zt[block] = (value * inverse).astype(jnp.bfloat16)


def early_kernel(matrix_own, matrix_near, matrix_far, *rest):
    texts, rest = rest[:2], rest[2:]
    zt, projected, turned, matrix, text, sems = rest
    depth, near = matrix_own.shape[0], matrix_near.shape[0]
    core, side = lax.rem(lax.axis_index("dp"), 2), lax.axis_index("fsdp")

    other = (1 - side) * depth
    places = (side * depth, other + core * near, other + (1 - core) * near)
    copies = []
    for k, (source, start) in enumerate(zip((matrix_own, matrix_near, matrix_far), places)):
        start = pl.multiple_of(start, 32)
        target = matrix.at[pl.ds(start, source.shape[0])]
        copies.append(pltpu.make_async_copy(source, target, sems.at[k]))
        copies[-1].start()
    count = texts[0].shape[0]
    for k, source in enumerate(texts):
        text[pl.ds(k * count, count)] = source[...]
    for s in (0, 1):

        @pl.when(side == s)
        def _():
            turned[...] = jnp.transpose(text[: turned.shape[1], s * depth : (s + 1) * depth])

    for copy in copies:
        copy.wait()
    project(text, matrix, projected, zt)


def batch_kernel(scalars, image, zt_early, projected_early, *rest):
    (turned_early, matrix), texts, images, rest = rest[:2], rest[2:6], rest[6:10], rest[10:]
    (grad_image, grad_text, head_grad), rest = rest[:3], rest[3:]
    zi, text, zt, projected, weights, grad, turned, proj, sems = rest
    rows = image.shape[0]
    total, width = zi.shape
    half = total // 2
    depth = head_grad.shape[0]
    group, side = lax.axis_index("dp"), lax.axis_index("fsdp")

    count = total // 4
    for sources, target in ((texts, text), (images, zi)):
        for k, source in enumerate(sources):
            target[pl.ds(k * count, count)] = source[:count]
    match = pair_indices(rows, total, images, side)
    late = pl.ds(half, half)
    project(text.at[late], matrix, projected.at[late], zt.at[late])
    zt[:half] = zt_early[...]
    first = turned_early.shape[1]
    turned[:, :first] = turned_early[...]
    for s in (0, 1):

        @pl.when(side == s)
        def _():
            turned[:, first:] = jnp.transpose(text[first:, s * depth : (s + 1) * depth])

    owner, row = owners(TEXT_ORDER, (total, 1), 0, rows, group * 2 + side)
    ids = owner * rows + row
    for cut in cuts(total, 256):
        scores = dot(zt[...], zi[cut], NT)
        weights[:, cut] = weigh(scores, ids == match[:, cut], scalars)
    for cut in cuts(width, 256):
        grad[:, cut] = dot(weights[...], zi[:, cut])
    for block in cuts(total, 160):
        value = projected_early[block] if block.stop <= half else projected[block]
        slope = grad[block]
        squares = jnp.sum(value * value, axis=1, keepdims=True) + epsilon
        inner = jnp.sum(value * slope, axis=1, keepdims=True)
        proj[block] = ((slope - value * (inner / squares)) * lax.rsqrt(squares)).astype(
            jnp.bfloat16
        )
    copies = []
    head = grad
    for k, cut in enumerate(cuts(width, 384)):
        head[:depth, cut] = dot(turned[...], proj[:, cut])
        copies.append(
            pltpu.make_async_copy(head.at[:depth, cut], head_grad.at[:, cut], sems.at[k])
        )
        copies[-1].start()
    grad_text[...] = dot(proj[:48], matrix[...], NT)[:rows]
    grad_zi = dot(weights[:, :128], zt[...], TN)[:rows]
    unit_image, image_norm = normalize(image[...].astype(jnp.float32))
    grad_image[...] = unproject(grad_zi, unit_image, image_norm)
    for copy in copies:
        copy.wait()


def gathered_plan(
    picture_mean_embeddings,
    caption_tower_summary,
    caption_mapping_matrix,
    picture_match_index,
    sharpness_factor,
    score_shift_term,
):
    rows, width = caption_tower_summary.shape
    depth = caption_mapping_matrix.shape[0]
    half = depth // 2
    total = rows * 32
    vmem = pl.BlockSpec(memory_space=pltpu.VMEM)
    anywhere = pl.BlockSpec(memory_space=pl.ANY)
    f32, bf16 = jnp.float32, jnp.bfloat16
    params = pltpu.CompilerParams(vmem_limit_bytes=24 * 2**20)

    hbm = pl.BlockSpec(memory_space=pltpu.HBM)
    own, quarter = pl.pallas_call(
        own_kernel,
        out_shape=(
            jax.ShapeDtypeStruct((2, rows + 4, width), bf16),
            jax.ShapeDtypeStruct((half, width), bf16),
        ),
        in_specs=[hbm] * 4,
        out_specs=(vmem, vmem),
        scratch_shapes=[
            pltpu.VMEM((rows, width), bf16),
            pltpu.VMEM((rows, width), bf16),
            pltpu.VMEM((1, 2 * rows), jnp.int32),
            pltpu.VMEM((8, width), f32),
            pltpu.SemaphoreType.DMA((4,)),
        ],
        name="own_block",
    )(
        picture_mean_embeddings,
        caption_tower_summary,
        caption_mapping_matrix,
        picture_match_index[None, :],
    )
    first = IMAGE_ORDER[1]
    blocks = [own, across(own, Y), across(own, first), across(own, first | Y)]
    near = across(quarter, Y)
    digits = [block[0, rows : rows + 2] for block in (blocks[0], blocks[2])]
    digits += [jnp.zeros((4, width), bf16)]
    images = jnp.concatenate([block[0, :rows] for block in blocks] + digits)
    texts = jnp.concatenate([block[1, :rows] for block in blocks])
    scalars = jnp.concatenate([sharpness_factor, score_shift_term])[None]
    texts, images, scalars = lax.optimization_barrier((texts, images, scalars))
    texts = jnp.concatenate([texts, across(texts, TEXT_ORDER[2])])
    count = 4 * rows
    beside = across(images, IMAGE_ORDER[2])
    digits = [images[count : count + 4], beside[count : count + 4]]
    images = jnp.concatenate([images[:count], beside[:count]] + digits)
    texts, images = lax.optimization_barrier((texts, images))
    texts = [texts, across(texts, CORE), across(texts, TEXT_ORDER[4])]
    images = [images, across(images, IMAGE_ORDER[3]), across(images, CORE)]
    near, texts[1] = lax.optimization_barrier((near, texts[1]))
    far = across(near, CORE)
    zt, projected, turned, matrix = pl.pallas_call(
        early_kernel,
        out_shape=(
            jax.ShapeDtypeStruct((total // 2, width), bf16),
            jax.ShapeDtypeStruct((total // 2, width), f32),
            jax.ShapeDtypeStruct((depth, 256), bf16),
            jax.ShapeDtypeStruct((2 * depth, width), bf16),
        ),
        in_specs=[anywhere] * 3 + [vmem] * 2,
        out_specs=(vmem,) * 4,
        scratch_shapes=[pltpu.VMEM((total // 2, width), bf16), pltpu.SemaphoreType.DMA((3,))],
        compiler_params=params,
        name="early_texts",
    )(caption_mapping_matrix, near, far, *texts[:2])
    texts.append(across(texts[2], CORE))
    images.append(across(images[1], CORE))
    return pl.pallas_call(
        batch_kernel,
        out_shape=(
            jax.ShapeDtypeStruct((rows, width), f32),
            jax.ShapeDtypeStruct((rows, width), f32),
            jax.ShapeDtypeStruct((depth, width), f32),
        ),
        in_specs=[vmem] * 14,
        out_specs=(vmem, vmem, anywhere),
        scratch_shapes=[
            pltpu.VMEM((total, width), bf16),
            pltpu.VMEM((total, width), bf16),
            pltpu.VMEM((total, width), bf16),
            pltpu.VMEM((total, width), f32),
            pltpu.VMEM((total, total), bf16),
            pltpu.VMEM((total, width), f32),
            pltpu.VMEM((depth, total), bf16),
            pltpu.VMEM((total, width), bf16),
            pltpu.SemaphoreType.DMA((8,)),
        ],
        compiler_params=params,
        name="batch",
    )(
        scalars,
        picture_mean_embeddings,
        zt,
        projected,
        turned,
        matrix,
        *texts,
        *images,
    )


def solution(mesh):
    gathered = dict(mesh.shape) == {"dp": 16, "fsdp": 2}
    per_device = gathered_plan if gathered else ring_plan
    return jax.shard_map(
        per_device,
        mesh=mesh,
        in_specs=(
            P(("dp", "fsdp"), None),
            P(("dp", "fsdp"), None),
            P("fsdp", None),
            P("dp"),
            P(),
            P(),
        ),
        out_specs=(P(("dp", "fsdp"), None), P(("dp", "fsdp"), None), P("fsdp", None)),
        check_vma=False,
    )
```

profile of v0, /device:TPU:0, one launch (start us, length us, event | category | flops | bytes accessed | tf_op | source)
XLA Modules:
  0.0 49.8 jit_solution(11069159399672466409)
XLA Ops:
  0.6 0.0 copy-start
  0.6 2.2 %own_block.1 = (bf16[2,24,1152]{2,1,0:T(8,128)(2,1)}, bf16[288,1152]{1,0:T(8,128)(2,1)}) custom-call(bf16[20,1152]{1,0:T(8,128)(2,1)} %image.3, bf16[20,1152]{1,0:T(8,128)(2,1)} %text.1, bf16[576,1152]{1,0:T(8,128)(2,1)} %matrix_own.1, s32[1,40]{1,0:T(1,128)} %bitcast.23), custom_call_target="tpu_custom_call" | custom-call | tf_op jit(solution)/shard_map/own_block/pallas_call | solution.py:289
  2.8 5.1 %collective-permute-start.2 = (bf16[2,24,1152]{2,1,0:T(8,128)(2,1)}, bf16[2,24,1152]{2,1,0:T(8,128)(2,1)S(1)}, u32[]{:S(2)}, u32[]{:S(2)}) collective-permute-start(bf16[2,24,1152]{2,1,0:T(8,128)(2,1)} %get-tuple-element.16), channel_id=1, source_target_pairs={{0,17},{1,16},{2,19},{3,18},{4,21},{5,20},{6,23},{7,22},{8,25},{9,... | collective-permute-start | bytes 331784 | tf_op jit(solution)/shard_map/ppermute | solution.py:107
  7.9 0.3 collective-permute-start.1
  8.2 0.3 collective-permute-start
  8.5 0.8 %slice_bitcast_fusion.9 = bf16[2,1152]{1,0:T(2,128)(2,1)S(1)} fusion(bf16[2,24,1152]{2,1,0:T(8,128)(2,1)} %get-tuple-element.16), kind=kLoop, calls=%fused_computation.12 | loop fusion | bytes 9216 | tf_op jit(solution)/shard_map/squeeze | solution.py:314
  9.3 0.8 %slice_bitcast_fusion.6 = (bf16[20,1152]{1,0:T(8,128)(2,1)S(1)}, bf16[20,1152]{1,0:T(8,128)(2,1)S(1)}) fusion(bf16[2,24,1152]{2,1,0:T(8,128)(2,1)} %get-tuple-element.16), kind=kLoop, calls=%fused_computation.9 | loop fusion | bytes 184320 | tf_op jit(solution)/shard_map/squeeze | solution.py:316
  11.4 0.1 maximum_bitcast_fusion.scalars
  11.5 5.2 %collective-permute-done.2 = bf16[2,24,1152]{2,1,0:T(8,128)(2,1)S(1)} collective-permute-done((bf16[2,24,1152]{2,1,0:T(8,128)(2,1)}, bf16[2,24,1152]{2,1,0:T(8,128)(2,1)S(1)}, u32[]{:S(2)}, u32[]{:S(2)}) %collective-permute-start.2) | collective-permute-done | bytes 110624 | tf_op jit(solution)/shard_map/ppermute | solution.py:107
  16.7 1.6 %collective-permute-done.1 = bf16[2,24,1152]{2,1,0:T(8,128)(2,1)S(1)} collective-permute-done((bf16[2,24,1152]{2,1,0:T(8,128)(2,1)}, bf16[2,24,1152]{2,1,0:T(8,128)(2,1)S(1)}, u32[]{:S(2)}, u32[]{:S(2)}) %collective-permute-start.1) | collective-permute-done | bytes 110624 | tf_op jit(solution)/shard_map/ppermute | solution.py:107
  18.3 0.0 collective-permute-done
  18.4 0.5 concatenate.16
  18.9 0.8 %collective-permute-start.4 = (bf16[80,1152]{1,0:T(8,128)(2,1)S(1)}, bf16[80,1152]{1,0:T(8,128)(2,1)S(1)}, u32[]{:S(2)}, u32[]{:S(2)}) collective-permute-start(bf16[80,1152]{1,0:T(8,128)(2,1)S(1)} %pad_maximum_fusion.2), channel_id=1, source_target_pairs={{0,8},{1,9},{2,10},{3,11},{4,12},{5,13},{6,14},{7,15},{8,0},{9,1},... | collective-permute-start | bytes 552968 | tf_op jit(solution)/shard_map/ppermute | solution.py:107
  19.8 0.5 %collective-permute-start.3 = (bf16[288,1152]{1,0:T(8,128)(2,1)}, bf16[288,1152]{1,0:T(8,128)(2,1)S(1)}, u32[]{:S(2)}, u32[]{:S(2)}) collective-permute-start(bf16[288,1152]{1,0:T(8,128)(2,1)} %get-tuple-element.18), channel_id=1, source_target_pairs={{0,1},{1,0},{2,3},{3,2},{4,5},{5,4},{6,7},{7,6},{8,9},{9,8},{10,11... | collective-permute-start | bytes 1990664 | tf_op jit(solution)/shard_map/ppermute | solution.py:107
  20.3 0.0 copy-start.1
  20.3 1.6 %collective-permute-start.5 = (bf16[88,1152]{1,0:T(8,128)(2,1)S(1)}, bf16[88,1152]{1,0:T(8,128)(2,1)S(1)}, u32[]{:S(2)}, u32[]{:S(2)}) collective-permute-start(bf16[88,1152]{1,0:T(8,128)(2,1)S(1)} %concatenate.16), channel_id=1, source_target_pairs={{0,4},{1,5},{2,6},{3,7},{4,0},{5,1},{6,2},{7,3},{8,12},{9,13},{10,... | collective-permute-start | bytes 608264 | tf_op jit(solution)/shard_map/ppermute | solution.py:107
  21.9 2.7 %collective-permute-done.4 = bf16[80,1152]{1,0:T(8,128)(2,1)S(1)} collective-permute-done((bf16[80,1152]{1,0:T(8,128)(2,1)S(1)}, bf16[80,1152]{1,0:T(8,128)(2,1)S(1)}, u32[]{:S(2)}, u32[]{:S(2)}) %collective-permute-start.4) | collective-permute-done | bytes 184352 | tf_op jit(solution)/shard_map/ppermute | solution.py:107
  24.6 2.2 %collective-permute-done.5 = bf16[88,1152]{1,0:T(8,128)(2,1)S(1)} collective-permute-done((bf16[88,1152]{1,0:T(8,128)(2,1)S(1)}, bf16[88,1152]{1,0:T(8,128)(2,1)S(1)}, u32[]{:S(2)}, u32[]{:S(2)}) %collective-permute-start.5) | collective-permute-done | bytes 202784 | tf_op jit(solution)/shard_map/ppermute | solution.py:107
  26.8 0.1 collective-permute-start.6
  26.9 0.7 %collective-permute-start.10 = (bf16[168,1152]{1,0:T(8,128)(2,1)S(1)}, bf16[168,1152]{1,0:T(8,128)(2,1)S(1)}, u32[]{:S(2)}, u32[]{:S(2)}) collective-permute-start(bf16[168,1152]{1,0:T(8,128)(2,1)S(1)} %pad_maximum_fusion.rest_6_), channel_id=1, source_target_pairs={{0,8},{1,9},{2,10},{3,11},{4,12},{5,13},{6,14},{7,15},{8,0},{9,1},... | collective-permute-start | bytes 1161224 | tf_op jit(solution)/shard_map/ppermute | solution.py:107
  27.6 1.5 %collective-permute-start.8 = (bf16[160,1152]{1,0:T(8,128)(2,1)S(1)}, bf16[160,1152]{1,0:T(8,128)(2,1)S(1)}, u32[]{:S(2)}, u32[]{:S(2)}) collective-permute-start(bf16[160,1152]{1,0:T(8,128)(2,1)S(1)} %pad_maximum_fusion.1.rest_0_.rest_2_), channel_id=1, source_target_pairs={{0,4},{1,5},{2,6},{3,7},{4,0},{5,1},{6,2},{7,3},{8,12},{9,13},{10,... | collective-permute-start | bytes 1105928 | tf_op jit(solution)/shard_map/ppermute | solution.py:107
  29.1 7.5 %collective-permute-done.3.matrix_near = bf16[288,1152]{1,0:T(8,128)(2,1)S(1)} collective-permute-done((bf16[288,1152]{1,0:T(8,128)(2,1)}, bf16[288,1152]{1,0:T(8,128)(2,1)S(1)}, u32[]{:S(2)}, u32[]{:S(2)}) %collective-permute-start.3) | collective-permute-done | bytes 663584 | tf_op jit(solution)/shard_map/ppermute | solution.py:107
  36.5 0.0 collective-permute-done.6.rest_1_.rest_3_
  36.5 0.0 collective-permute-start.7
  36.5 0.5 %collective-permute-start.11 = (bf16[168,1152]{1,0:T(8,128)(2,1)S(1)}, bf16[168,1152]{1,0:T(8,128)(2,1)S(1)}, u32[]{:S(2)}, u32[]{:S(2)}) collective-permute-start(bf16[168,1152]{1,0:T(8,128)(2,1)S(1)} %pad_maximum_fusion.rest_6_), channel_id=1, source_target_pairs={{0,2},{1,3},{2,0},{3,1},{4,6},{5,7},{6,4},{7,5},{8,10},{9,11},{10,... | collective-permute-start | bytes 1161224 | tf_op jit(solution)/shard_map/ppermute | solution.py:107
  37.0 1.3 %collective-permute-done.10.rest_7_ = bf16[168,1152]{1,0:T(8,128)(2,1)S(1)} collective-permute-done((bf16[168,1152]{1,0:T(8,128)(2,1)S(1)}, bf16[168,1152]{1,0:T(8,128)(2,1)S(1)}, u32[]{:S(2)}, u32[]{:S(2)}) %collective-permute-start.10) | collective-permute-done | bytes 387104 | tf_op jit(solution)/shard_map/ppermute | solution.py:107
  38.3 0.0 collective-permute-start.12
  38.3 0.0 collective-permute-done.8.rest_4_
  38.3 0.5 %collective-permute-start.9 = (bf16[160,1152]{1,0:T(8,128)(2,1)S(1)}, bf16[160,1152]{1,0:T(8,128)(2,1)S(1)}, u32[]{:S(2)}, u32[]{:S(2)}) collective-permute-start(bf16[160,1152]{1,0:T(8,128)(2,1)S(1)} %collective-permute-done.8.rest_4_), channel_id=1, source_target_pairs={{0,2},{1,3},{2,0},{3,1},{4,6},{5,7},{6,4},{7,5},{8,10},{9,11},{10,... | collective-permute-start | bytes 1105928 | tf_op jit(solution)/shard_map/ppermute | solution.py:107
  38.8 0.0 collective-permute-done.7.matrix_far
  38.8 0.0 copy-done
  38.8 2.1 %early_texts.1 = (bf16[320,1152]{1,0:T(8,128)(2,1)S(1)}, f32[320,1152]{1,0:T(8,128)S(1)}, bf16[576,256]{1,0:T(8,128)(2,1)S(1)}, bf16[1152,1152]{1,0:T(8,128)(2,1)S(1)}) custom-call(bf16[576,1152]{1,0:T(8,128)(2,1)S(1)} %copy-done, bf16[288,1152]{1,0:T(8,128)(2,1)S(1)} %collective-permute-done.3.matrix_near, ...), custom_call_target="tpu_custom_call" | custom-call | tf_op jit(solution)/shard_map/early_texts/pallas_call | solution.py:330
  41.0 0.0 collective-permute-done.11.rest_8_
  41.0 0.0 collective-permute-done.9.rest_5_
  41.0 0.0 collective-permute-done.12.rest_9_
  41.0 0.0 copy-done.1
  41.0 8.7 %batch.1 = (f32[20,1152]{1,0:T(8,128)}, f32[20,1152]{1,0:T(8,128)}, f32[576,1152]{1,0:T(8,128)}) custom-call(f32[1,2]{1,0:T(1,128)S(1)} %maximum_bitcast_fusion.scalars, bf16[20,1152]{1,0:T(8,128)(2,1)S(1)} %copy-done.1, bf16[320,1152]{1,0:T(8,128)(2,1)S(1)} %get-tuple-element.24.zt_early, f32[320,1152]{1,0:T(8,128)S(1)} %get-tuple-element.25.projected_early, ...), custom_call_target="tpu_custom_call" | custom-call | tf_op jit(solution)/shard_map/batch/pallas_call | solution.py:346
  (12 shorter events, 0.2 us)
Async XLA Ops:
  0.6 38.2 %copy-start = (bf16[576,1152]{1,0:T(8,128)(2,1)S(1)}, bf16[576,1152]{1,0:T(8,128)(2,1)}, u32[]{:S(2)}) copy-start(bf16[576,1152]{1,0:T(8,128)(2,1)} %matrix_own.1) | copy-start | bytes 3981316
  2.8 13.9 %collective-permute-start.2 = (bf16[2,24,1152]{2,1,0:T(8,128)(2,1)}, bf16[2,24,1152]{2,1,0:T(8,128)(2,1)S(1)}, u32[]{:S(2)}, u32[]{:S(2)}) collective-permute-start(bf16[2,24,1152]{2,1,0:T(8,128)(2,1)} %get-tuple-element.16), channel_id=1, source_target_pairs={{0,17},{1,16},{2,19},{3,18},{4,21},{5,20},{6,23},{7,22},{8,25},{9,... | collective-permute-start | bytes 331784 | tf_op jit(solution)/shard_map/ppermute | solution.py:107
  7.9 10.4 %collective-permute-start.1 = (bf16[2,24,1152]{2,1,0:T(8,128)(2,1)}, bf16[2,24,1152]{2,1,0:T(8,128)(2,1)S(1)}, u32[]{:S(2)}, u32[]{:S(2)}) collective-permute-start(bf16[2,24,1152]{2,1,0:T(8,128)(2,1)} %get-tuple-element.16), channel_id=1, source_target_pairs={{0,16},{1,17},{2,18},{3,19},{4,20},{5,21},{6,22},{7,23},{8,24},{9,... | collective-permute-start | bytes 331784 | tf_op jit(solution)/shard_map/ppermute | solution.py:107
  8.2 10.1 %collective-permute-start = (bf16[2,24,1152]{2,1,0:T(8,128)(2,1)}, bf16[2,24,1152]{2,1,0:T(8,128)(2,1)S(1)}, u32[]{:S(2)}, u32[]{:S(2)}) collective-permute-start(bf16[2,24,1152]{2,1,0:T(8,128)(2,1)} %get-tuple-element.16), channel_id=1, source_target_pairs={{0,1},{1,0},{2,3},{3,2},{4,5},{5,4},{6,7},{7,6},{8,9},{9,8},{10,11... | collective-permute-start | bytes 331784 | tf_op jit(solution)/shard_map/ppermute | solution.py:107
  18.9 5.7 %collective-permute-start.4 = (bf16[80,1152]{1,0:T(8,128)(2,1)S(1)}, bf16[80,1152]{1,0:T(8,128)(2,1)S(1)}, u32[]{:S(2)}, u32[]{:S(2)}) collective-permute-start(bf16[80,1152]{1,0:T(8,128)(2,1)S(1)} %pad_maximum_fusion.2), channel_id=1, source_target_pairs={{0,8},{1,9},{2,10},{3,11},{4,12},{5,13},{6,14},{7,15},{8,0},{9,1},... | collective-permute-start | bytes 552968 | tf_op jit(solution)/shard_map/ppermute | solution.py:107
  19.8 16.8 %collective-permute-start.3 = (bf16[288,1152]{1,0:T(8,128)(2,1)}, bf16[288,1152]{1,0:T(8,128)(2,1)S(1)}, u32[]{:S(2)}, u32[]{:S(2)}) collective-permute-start(bf16[288,1152]{1,0:T(8,128)(2,1)} %get-tuple-element.18), channel_id=1, source_target_pairs={{0,1},{1,0},{2,3},{3,2},{4,5},{5,4},{6,7},{7,6},{8,9},{9,8},{10,11... | collective-permute-start | bytes 1990664 | tf_op jit(solution)/shard_map/ppermute | solution.py:107
  20.3 20.7 %copy-start.1 = (bf16[20,1152]{1,0:T(8,128)(2,1)S(1)}, bf16[20,1152]{1,0:T(8,128)(2,1)}, u32[]{:S(2)}) copy-start(bf16[20,1152]{1,0:T(8,128)(2,1)} %image.3) | copy-start | bytes 138244
  20.3 6.5 %collective-permute-start.5 = (bf16[88,1152]{1,0:T(8,128)(2,1)S(1)}, bf16[88,1152]{1,0:T(8,128)(2,1)S(1)}, u32[]{:S(2)}, u32[]{:S(2)}) collective-permute-start(bf16[88,1152]{1,0:T(8,128)(2,1)S(1)} %concatenate.16), channel_id=1, source_target_pairs={{0,4},{1,5},{2,6},{3,7},{4,0},{5,1},{6,2},{7,3},{8,12},{9,13},{10,... | collective-permute-start | bytes 608264 | tf_op jit(solution)/shard_map/ppermute | solution.py:107
  26.8 9.7 %collective-permute-start.6 = (bf16[160,1152]{1,0:T(8,128)(2,1)S(1)}, bf16[160,1152]{1,0:T(8,128)(2,1)S(1)}, u32[]{:S(2)}, u32[]{:S(2)}) collective-permute-start(bf16[160,1152]{1,0:T(8,128)(2,1)S(1)} %pad_maximum_fusion.1.rest_0_.rest_2_), channel_id=1, source_target_pairs={{0,2},{1,3},{2,0},{3,1},{4,6},{5,7},{6,4},{7,5},{8,10},{9,11},{10,... | collective-permute-start | bytes 1105928 | tf_op jit(solution)/shard_map/ppermute | solution.py:107
  26.9 11.4 %collective-permute-start.10 = (bf16[168,1152]{1,0:T(8,128)(2,1)S(1)}, bf16[168,1152]{1,0:T(8,128)(2,1)S(1)}, u32[]{:S(2)}, u32[]{:S(2)}) collective-permute-start(bf16[168,1152]{1,0:T(8,128)(2,1)S(1)} %pad_maximum_fusion.rest_6_), channel_id=1, source_target_pairs={{0,8},{1,9},{2,10},{3,11},{4,12},{5,13},{6,14},{7,15},{8,0},{9,1},... | collective-permute-start | bytes 1161224 | tf_op jit(solution)/shard_map/ppermute | solution.py:107
  27.6 10.7 %collective-permute-start.8 = (bf16[160,1152]{1,0:T(8,128)(2,1)S(1)}, bf16[160,1152]{1,0:T(8,128)(2,1)S(1)}, u32[]{:S(2)}, u32[]{:S(2)}) collective-permute-start(bf16[160,1152]{1,0:T(8,128)(2,1)S(1)} %pad_maximum_fusion.1.rest_0_.rest_2_), channel_id=1, source_target_pairs={{0,4},{1,5},{2,6},{3,7},{4,0},{5,1},{6,2},{7,3},{8,12},{9,13},{10,... | collective-permute-start | bytes 1105928 | tf_op jit(solution)/shard_map/ppermute | solution.py:107
  36.5 2.3 %collective-permute-start.7 = (bf16[288,1152]{1,0:T(8,128)(2,1)S(1)}, bf16[288,1152]{1,0:T(8,128)(2,1)S(1)}, u32[]{:S(2)}, u32[]{:S(2)}) collective-permute-start(bf16[288,1152]{1,0:T(8,128)(2,1)S(1)} %collective-permute-done.3.matrix_near), channel_id=1, source_target_pairs={{0,2},{1,3},{2,0},{3,1},{4,6},{5,7},{6,4},{7,5},{8,10},{9,11},{10,... | collective-permute-start | bytes 1990664 | tf_op jit(solution)/shard_map/ppermute | solution.py:107
  36.5 4.5 %collective-permute-start.11 = (bf16[168,1152]{1,0:T(8,128)(2,1)S(1)}, bf16[168,1152]{1,0:T(8,128)(2,1)S(1)}, u32[]{:S(2)}, u32[]{:S(2)}) collective-permute-start(bf16[168,1152]{1,0:T(8,128)(2,1)S(1)} %pad_maximum_fusion.rest_6_), channel_id=1, source_target_pairs={{0,2},{1,3},{2,0},{3,1},{4,6},{5,7},{6,4},{7,5},{8,10},{9,11},{10,... | collective-permute-start | bytes 1161224 | tf_op jit(solution)/shard_map/ppermute | solution.py:107
  38.3 2.7 %collective-permute-start.12 = (bf16[168,1152]{1,0:T(8,128)(2,1)S(1)}, bf16[168,1152]{1,0:T(8,128)(2,1)S(1)}, u32[]{:S(2)}, u32[]{:S(2)}) collective-permute-start(bf16[168,1152]{1,0:T(8,128)(2,1)S(1)} %collective-permute-done.10.rest_7_), channel_id=1, source_target_pairs={{0,2},{1,3},{2,0},{3,1},{4,6},{5,7},{6,4},{7,5},{8,10},{9,11},{10,... | collective-permute-start | bytes 1161224 | tf_op jit(solution)/shard_map/ppermute | solution.py:107
  38.3 2.7 %collective-permute-start.9 = (bf16[160,1152]{1,0:T(8,128)(2,1)S(1)}, bf16[160,1152]{1,0:T(8,128)(2,1)S(1)}, u32[]{:S(2)}, u32[]{:S(2)}) collective-permute-start(bf16[160,1152]{1,0:T(8,128)(2,1)S(1)} %collective-permute-done.8.rest_4_), channel_id=1, source_target_pairs={{0,2},{1,3},{2,0},{3,1},{4,6},{5,7},{6,4},{7,5},{8,10},{9,11},{10,... | collective-permute-start | bytes 1105928 | tf_op jit(solution)/shard_map/ppermute | solution.py:107
where the time goes:
time: 50 us; the launch traced here: 49.8 us
  waiting for transfers between devices  20.4 us (41%)
  Pallas kernels  13.1 us (26%)
  starting transfers between devices  11.8 us (24%)
  local copies, waits for them, and re-layouts  2.2 us (4%)
  between operations  2.08 us (4%)
    ppermute x13, waiting for transfers between devices, across(): lax.ppermute(block, ('dp', 'fsdp'), [(i, i ^ bits) for i in range(count)])  20.4 us
    ppermute x13, starting transfers between devices, across(): lax.ppermute(block, ('dp', 'fsdp'), [(i, i ^ bits) for i in range(count)])  11.8 us
    pallas_call x1, Pallas kernels, gathered_plan(): pl.pallas_call(batch_kernel, out_shape=(jax.ShapeDtypeStruct((rows, width...  8.73 us
    pallas_call x1, Pallas kernels, gathered_plan(): pl.pallas_call(own_kernel, out_shape=(jax.ShapeDtypeStruct((2, rows + 4,...  2.18 us
    pallas_call x1, Pallas kernels, gathered_plan(): pl.pallas_call(early_kernel, out_shape=(jax.ShapeDtypeStruct((total // 2,...  2.14 us
  transfers between devices with their start and end apart: 13, of which 6 were waited for; matrix products, arithmetic and copies ran while one was open for 4% of the time, Pallas kernels for 4%

commit v1 on v0

--- a/solution.py
+++ b/solution.py
@@ -138,7 +138,8 @@
     return (jnp.where(paired, -sharpness, sharpness) * share).astype(jnp.bfloat16)
 
 
-def own_kernel(image, text, matrix, match, own, quarter, images, texts, indices, digits, sems):
+def own_kernel(image, text, matrix, match, own, plain, quarter, *rest):
+    images, texts, indices, digits, sems = rest
     rows = images.shape[0]
     count = quarter.shape[0]
     start = pl.multiple_of(lax.rem(lax.axis_index("dp"), 2) * count, 32)
@@ -158,6 +159,7 @@
     own[0] = jnp.concatenate([unit_image, spare]).astype(jnp.bfloat16)
     text_rows = texts[...].astype(jnp.float32)
     own[1] = jnp.concatenate([text_rows, jnp.zeros_like(spare)]).astype(jnp.bfloat16)
+    plain[...] = jnp.concatenate([unit_image, text_rows]).astype(jnp.bfloat16)
     copies[3].wait()
 
 
@@ -286,14 +288,15 @@
     params = pltpu.CompilerParams(vmem_limit_bytes=24 * 2**20)
 
     hbm = pl.BlockSpec(memory_space=pltpu.HBM)
-    own, quarter = pl.pallas_call(
+    own, plain, quarter = pl.pallas_call(
         own_kernel,
         out_shape=(
             jax.ShapeDtypeStruct((2, rows + 4, width), bf16),
+            jax.ShapeDtypeStruct((2 * rows, width), bf16),
             jax.ShapeDtypeStruct((half, width), bf16),
         ),
         in_specs=[hbm] * 4,
-        out_specs=(vmem, vmem),
+        out_specs=(vmem, vmem, vmem),
         scratch_shapes=[
             pltpu.VMEM((rows, width), bf16),
             pltpu.VMEM((rows, width), bf16),
@@ -309,12 +312,15 @@
         picture_match_index[None, :],
     )
     first = IMAGE_ORDER[1]
-    blocks = [own, across(own, Y), across(own, first), across(own, first | Y)]
+    beside = across(own, first)
+    blocks = [plain, across(plain, Y), beside, across(plain, first | Y)]
     near = across(quarter, Y)
-    digits = [block[0, rows : rows + 2] for block in (blocks[0], blocks[2])]
+    digits = [block[0, rows : rows + 2] for block in (own, beside)]
     digits += [jnp.zeros((4, width), bf16)]
-    images = jnp.concatenate([block[0, :rows] for block in blocks] + digits)
-    texts = jnp.concatenate([block[1, :rows] for block in blocks])
+    images = [block[0, :rows] if block is beside else block[:rows] for block in blocks]
+    images = jnp.concatenate(images + digits)
+    texts = [block[1, :rows] if block is beside else block[rows:] for block in blocks]
+    texts = jnp.concatenate(texts)
     scalars = jnp.concatenate([sharpness_factor, score_shift_term])[None]
     texts, images, scalars = lax.optimization_barrier((texts, images, scalars))
     texts = jnp.concatenate([texts, across(texts, TEXT_ORDER[2])])

time: 50 us -> 49.2 us (0.984)
  waiting for transfers between devices: 20.4 us -> 19.4 us
    ppermute x13, waiting for transfers between devices: 20.4 us -> 19.4 us  [across(): lax.ppermute(block, ('dp', 'fsdp'), [(i, i ^ bits) for i in range(count)])]
    slice x0 -> x3, local copies, waits for them, and re-layouts: none -> 0.94 us  [gathered_plan(): block[:rows]]
    squeeze x6 -> x3, local copies, waits for them, and re-layouts: 1.65 us -> 0.78 us  [the longest x2 0.77 us: gathered_plan(): digits = [block[0, rows:rows + 2] for block in (own, beside)]]
  transfers between devices with their start and end apart: 13 -> 13, of which waited for: 6 -> 7; matrix products, arithmetic and copies ran while one was open for 4% -> 4% of each run, Pallas kernels for 4% -> 4%
where the time goes in v1:
time: 49.2 us; the launch traced here: 48.9 us
  waiting for transfers between devices  19.4 us (39%)
  Pallas kernels  13.1 us (27%)
  starting transfers between devices  11.9 us (24%)
  local copies, waits for them, and re-layouts  2.27 us (5%)
  between operations  2.06 us (4%)
    ppermute x13, waiting for transfers between devices, across(): lax.ppermute(block, ('dp', 'fsdp'), [(i, i ^ bits) for i in range(count)])  19.4 us
    ppermute x13, starting transfers between devices, across(): lax.ppermute(block, ('dp', 'fsdp'), [(i, i ^ bits) for i in range(count)])  11.9 us
    pallas_call x1, Pallas kernels, gathered_plan(): pl.pallas_call(batch_kernel, out_shape=(jax.ShapeDtypeStruct((rows, width...  8.75 us
    pallas_call x1, Pallas kernels, gathered_plan(): pl.pallas_call(own_kernel, out_shape=(jax.ShapeDtypeStruct((2, rows + 4,...  2.21 us
    pallas_call x1, Pallas kernels, gathered_plan(): pl.pallas_call(early_kernel, out_shape=(jax.ShapeDtypeStruct((total // 2,...  2.14 us
  transfers between devices with their start and end apart: 13, of which 7 were waited for; matrix products, arithmetic and copies ran while one was open for 4% of the time, Pallas kernels for 4%

profile of v1, /device:TPU:0, one launch (start us, length us, event | category | flops | bytes accessed | tf_op | source)
XLA Modules:
  0.0 48.9 jit_solution(11393913598139336043)
XLA Ops:
  0.6 0.0 copy-start
  0.6 2.2 %own_block.1 = (bf16[2,24,1152]{2,1,0:T(8,128)(2,1)}, bf16[40,1152]{1,0:T(8,128)(2,1)}, bf16[288,1152]{1,0:T(8,128)(2,1)}) custom-call(bf16[20,1152]{1,0:T(8,128)(2,1)} %image.3, bf16[20,1152]{1,0:T(8,128)(2,1)} %text.1, bf16[576,1152]{1,0:T(8,128)(2,1)} %matrix_own.1, s32[1,40]{1,0:T(1,128)} %bitcast.11), custom_call_target="tpu_custom_call" | custom-call | tf_op jit(solution)/shard_map/own_block/pallas_call | solution.py:291
  2.9 5.1 %collective-permute-start.2 = (bf16[40,1152]{1,0:T(8,128)(2,1)}, bf16[40,1152]{1,0:T(8,128)(2,1)S(1)}, u32[]{:S(2)}, u32[]{:S(2)}) collective-permute-start(bf16[40,1152]{1,0:T(8,128)(2,1)} %get-tuple-element.17), channel_id=1, source_target_pairs={{0,17},{1,16},{2,19},{3,18},{4,21},{5,20},{6,23},{7,22},{8,25},{9,... | collective-permute-start | bytes 276488 | tf_op jit(solution)/shard_map/ppermute | solution.py:107
  7.9 0.5 %collective-permute-start = (bf16[40,1152]{1,0:T(8,128)(2,1)}, bf16[40,1152]{1,0:T(8,128)(2,1)S(1)}, u32[]{:S(2)}, u32[]{:S(2)}) collective-permute-start(bf16[40,1152]{1,0:T(8,128)(2,1)} %get-tuple-element.17), channel_id=1, source_target_pairs={{0,1},{1,0},{2,3},{3,2},{4,5},{5,4},{6,7},{7,6},{8,9},{9,8},{10,11... | collective-permute-start | bytes 276488 | tf_op jit(solution)/shard_map/ppermute | solution.py:107
  8.4 0.1 collective-permute-start.1
  8.6 0.8 %slice_bitcast_fusion.3 = bf16[2,1152]{1,0:T(2,128)(2,1)S(1)} fusion(bf16[2,24,1152]{2,1,0:T(8,128)(2,1)} %get-tuple-element.18), kind=kLoop, calls=%fused_computation.6 | loop fusion | bytes 9216 | tf_op jit(solution)/shard_map/squeeze | solution.py:318
  9.3 0.9 %fusion.2 = (bf16[20,1152]{1,0:T(8,128)(2,1)S(1)}, bf16[20,1152]{1,0:T(8,128)(2,1)S(1)}) fusion(bf16[40,1152]{1,0:T(8,128)(2,1)} %get-tuple-element.17), kind=kLoop, calls=%fused_computation.10 | loop fusion | bytes 184320 | tf_op jit(solution)/shard_map/slice | solution.py:320
  11.5 0.1 maximum_bitcast_fusion.scalars
  11.6 1.5 %collective-permute-done.2 = bf16[40,1152]{1,0:T(8,128)(2,1)S(1)} collective-permute-done((bf16[40,1152]{1,0:T(8,128)(2,1)}, bf16[40,1152]{1,0:T(8,128)(2,1)S(1)}, u32[]{:S(2)}, u32[]{:S(2)}) %collective-permute-start.2) | collective-permute-done | bytes 92192 | tf_op jit(solution)/shard_map/ppermute | solution.py:107
  13.1 0.4 collective-permute-done
  13.5 4.1 %collective-permute-done.1 = bf16[2,24,1152]{2,1,0:T(8,128)(2,1)S(1)} collective-permute-done((bf16[2,24,1152]{2,1,0:T(8,128)(2,1)}, bf16[2,24,1152]{2,1,0:T(8,128)(2,1)S(1)}, u32[]{:S(2)}, u32[]{:S(2)}) %collective-permute-start.1) | collective-permute-done | bytes 110624 | tf_op jit(solution)/shard_map/ppermute | solution.py:107
  17.7 0.5 concatenate.16
  18.2 0.8 %collective-permute-start.4 = (bf16[80,1152]{1,0:T(8,128)(2,1)S(1)}, bf16[80,1152]{1,0:T(8,128)(2,1)S(1)}, u32[]{:S(2)}, u32[]{:S(2)}) collective-permute-start(bf16[80,1152]{1,0:T(8,128)(2,1)S(1)} %pad_maximum_fusion.2), channel_id=1, source_target_pairs={{0,8},{1,9},{2,10},{3,11},{4,12},{5,13},{6,14},{7,15},{8,0},{9,1},... | collective-permute-start | bytes 552968 | tf_op jit(solution)/shard_map/ppermute | solution.py:107
  19.0 0.5 %collective-permute-start.3 = (bf16[288,1152]{1,0:T(8,128)(2,1)}, bf16[288,1152]{1,0:T(8,128)(2,1)S(1)}, u32[]{:S(2)}, u32[]{:S(2)}) collective-permute-start(bf16[288,1152]{1,0:T(8,128)(2,1)} %get-tuple-element.20), channel_id=1, source_target_pairs={{0,1},{1,0},{2,3},{3,2},{4,5},{5,4},{6,7},{7,6},{8,9},{9,8},{10,11... | collective-permute-start | bytes 1990664 | tf_op jit(solution)/shard_map/ppermute | solution.py:107
  19.5 0.0 copy-start.1
  19.5 1.6 %collective-permute-start.5 = (bf16[88,1152]{1,0:T(8,128)(2,1)S(1)}, bf16[88,1152]{1,0:T(8,128)(2,1)S(1)}, u32[]{:S(2)}, u32[]{:S(2)}) collective-permute-start(bf16[88,1152]{1,0:T(8,128)(2,1)S(1)} %concatenate.16), channel_id=1, source_target_pairs={{0,4},{1,5},{2,6},{3,7},{4,0},{5,1},{6,2},{7,3},{8,12},{9,13},{10,... | collective-permute-start | bytes 608264 | tf_op jit(solution)/shard_map/ppermute | solution.py:107
  21.1 3.0 %collective-permute-done.4 = bf16[80,1152]{1,0:T(8,128)(2,1)S(1)} collective-permute-done((bf16[80,1152]{1,0:T(8,128)(2,1)S(1)}, bf16[80,1152]{1,0:T(8,128)(2,1)S(1)}, u32[]{:S(2)}, u32[]{:S(2)}) %collective-permute-start.4) | collective-permute-done | bytes 184352 | tf_op jit(solution)/shard_map/ppermute | solution.py:107
  24.1 1.9 %collective-permute-done.5 = bf16[88,1152]{1,0:T(8,128)(2,1)S(1)} collective-permute-done((bf16[88,1152]{1,0:T(8,128)(2,1)S(1)}, bf16[88,1152]{1,0:T(8,128)(2,1)S(1)}, u32[]{:S(2)}, u32[]{:S(2)}) %collective-permute-start.5) | collective-permute-done | bytes 202784 | tf_op jit(solution)/shard_map/ppermute | solution.py:107
  26.0 0.1 collective-permute-start.6
  26.1 0.7 %collective-permute-start.10 = (bf16[168,1152]{1,0:T(8,128)(2,1)S(1)}, bf16[168,1152]{1,0:T(8,128)(2,1)S(1)}, u32[]{:S(2)}, u32[]{:S(2)}) collective-permute-start(bf16[168,1152]{1,0:T(8,128)(2,1)S(1)} %pad_maximum_fusion.rest_6_), channel_id=1, source_target_pairs={{0,8},{1,9},{2,10},{3,11},{4,12},{5,13},{6,14},{7,15},{8,0},{9,1},... | collective-permute-start | bytes 1161224 | tf_op jit(solution)/shard_map/ppermute | solution.py:107
  26.8 1.5 %collective-permute-start.8 = (bf16[160,1152]{1,0:T(8,128)(2,1)S(1)}, bf16[160,1152]{1,0:T(8,128)(2,1)S(1)}, u32[]{:S(2)}, u32[]{:S(2)}) collective-permute-start(bf16[160,1152]{1,0:T(8,128)(2,1)S(1)} %pad_maximum_fusion.1.rest_0_.rest_2_), channel_id=1, source_target_pairs={{0,4},{1,5},{2,6},{3,7},{4,0},{5,1},{6,2},{7,3},{8,12},{9,13},{10,... | collective-permute-start | bytes 1105928 | tf_op jit(solution)/shard_map/ppermute | solution.py:107
  28.3 7.4 %collective-permute-done.3.matrix_near = bf16[288,1152]{1,0:T(8,128)(2,1)S(1)} collective-permute-done((bf16[288,1152]{1,0:T(8,128)(2,1)}, bf16[288,1152]{1,0:T(8,128)(2,1)S(1)}, u32[]{:S(2)}, u32[]{:S(2)}) %collective-permute-start.3) | collective-permute-done | bytes 663584 | tf_op jit(solution)/shard_map/ppermute | solution.py:107
  35.7 0.0 collective-permute-done.6.rest_1_.rest_3_
  35.7 0.0 collective-permute-start.7
  35.7 0.5 %collective-permute-start.11 = (bf16[168,1152]{1,0:T(8,128)(2,1)S(1)}, bf16[168,1152]{1,0:T(8,128)(2,1)S(1)}, u32[]{:S(2)}, u32[]{:S(2)}) collective-permute-start(bf16[168,1152]{1,0:T(8,128)(2,1)S(1)} %pad_maximum_fusion.rest_6_), channel_id=1, source_target_pairs={{0,2},{1,3},{2,0},{3,1},{4,6},{5,7},{6,4},{7,5},{8,10},{9,11},{10,... | collective-permute-start | bytes 1161224 | tf_op jit(solution)/shard_map/ppermute | solution.py:107
  36.3 1.2 %collective-permute-done.10.rest_7_ = bf16[168,1152]{1,0:T(8,128)(2,1)S(1)} collective-permute-done((bf16[168,1152]{1,0:T(8,128)(2,1)S(1)}, bf16[168,1152]{1,0:T(8,128)(2,1)S(1)}, u32[]{:S(2)}, u32[]{:S(2)}) %collective-permute-start.10) | collective-permute-done | bytes 387104 | tf_op jit(solution)/shard_map/ppermute | solution.py:107
  37.5 0.0 collective-permute-start.12
  37.5 0.0 collective-permute-done.8.rest_4_
  37.5 0.5 %collective-permute-start.9 = (bf16[160,1152]{1,0:T(8,128)(2,1)S(1)}, bf16[160,1152]{1,0:T(8,128)(2,1)S(1)}, u32[]{:S(2)}, u32[]{:S(2)}) collective-permute-start(bf16[160,1152]{1,0:T(8,128)(2,1)S(1)} %collective-permute-done.8.rest_4_), channel_id=1, source_target_pairs={{0,2},{1,3},{2,0},{3,1},{4,6},{5,7},{6,4},{7,5},{8,10},{9,11},{10,... | collective-permute-start | bytes 1105928 | tf_op jit(solution)/shard_map/ppermute | solution.py:107
  38.0 0.0 collective-permute-done.7.matrix_far
  38.0 0.0 copy-done
  38.0 2.1 %early_texts.1 = (bf16[320,1152]{1,0:T(8,128)(2,1)S(1)}, f32[320,1152]{1,0:T(8,128)S(1)}, bf16[576,256]{1,0:T(8,128)(2,1)S(1)}, bf16[1152,1152]{1,0:T(8,128)(2,1)S(1)}) custom-call(bf16[576,1152]{1,0:T(8,128)(2,1)S(1)} %copy-done, bf16[288,1152]{1,0:T(8,128)(2,1)S(1)} %collective-permute-done.3.matrix_near, ...), custom_call_target="tpu_custom_call" | custom-call | tf_op jit(solution)/shard_map/early_texts/pallas_call | solution.py:336
  40.2 0.0 collective-permute-done.11.rest_8_
  40.2 0.0 collective-permute-done.9.rest_5_
  40.2 0.0 collective-permute-done.12.rest_9_
  40.2 0.0 copy-done.1
  40.2 8.7 %batch.1 = (f32[20,1152]{1,0:T(8,128)}, f32[20,1152]{1,0:T(8,128)}, f32[576,1152]{1,0:T(8,128)}) custom-call(f32[1,2]{1,0:T(1,128)S(1)} %maximum_bitcast_fusion.scalars, bf16[20,1152]{1,0:T(8,128)(2,1)S(1)} %copy-done.1, bf16[320,1152]{1,0:T(8,128)(2,1)S(1)} %get-tuple-element.26.zt_early, f32[320,1152]{1,0:T(8,128)S(1)} %get-tuple-element.27.projected_early, ...), custom_call_target="tpu_custom_call" | custom-call | tf_op jit(solution)/shard_map/batch/pallas_call | solution.py:352
  (12 shorter events, 0.2 us)
Async XLA Ops:
  0.6 37.4 %copy-start = (bf16[576,1152]{1,0:T(8,128)(2,1)S(1)}, bf16[576,1152]{1,0:T(8,128)(2,1)}, u32[]{:S(2)}) copy-start(bf16[576,1152]{1,0:T(8,128)(2,1)} %matrix_own.1) | copy-start | bytes 3981316
  2.9 10.2 %collective-permute-start.2 = (bf16[40,1152]{1,0:T(8,128)(2,1)}, bf16[40,1152]{1,0:T(8,128)(2,1)S(1)}, u32[]{:S(2)}, u32[]{:S(2)}) collective-permute-start(bf16[40,1152]{1,0:T(8,128)(2,1)} %get-tuple-element.17), channel_id=1, source_target_pairs={{0,17},{1,16},{2,19},{3,18},{4,21},{5,20},{6,23},{7,22},{8,25},{9,... | collective-permute-start | bytes 276488 | tf_op jit(solution)/shard_map/ppermute | solution.py:107
  7.9 5.6 %collective-permute-start = (bf16[40,1152]{1,0:T(8,128)(2,1)}, bf16[40,1152]{1,0:T(8,128)(2,1)S(1)}, u32[]{:S(2)}, u32[]{:S(2)}) collective-permute-start(bf16[40,1152]{1,0:T(8,128)(2,1)} %get-tuple-element.17), channel_id=1, source_target_pairs={{0,1},{1,0},{2,3},{3,2},{4,5},{5,4},{6,7},{7,6},{8,9},{9,8},{10,11... | collective-permute-start | bytes 276488 | tf_op jit(solution)/shard_map/ppermute | solution.py:107
  8.4 9.2 %collective-permute-start.1 = (bf16[2,24,1152]{2,1,0:T(8,128)(2,1)}, bf16[2,24,1152]{2,1,0:T(8,128)(2,1)S(1)}, u32[]{:S(2)}, u32[]{:S(2)}) collective-permute-start(bf16[2,24,1152]{2,1,0:T(8,128)(2,1)} %get-tuple-element.18), channel_id=1, source_target_pairs={{0,16},{1,17},{2,18},{3,19},{4,20},{5,21},{6,22},{7,23},{8,24},{9,... | collective-permute-start | bytes 331784 | tf_op jit(solution)/shard_map/ppermute | solution.py:107
  18.2 5.9 %collective-permute-start.4 = (bf16[80,1152]{1,0:T(8,128)(2,1)S(1)}, bf16[80,1152]{1,0:T(8,128)(2,1)S(1)}, u32[]{:S(2)}, u32[]{:S(2)}) collective-permute-start(bf16[80,1152]{1,0:T(8,128)(2,1)S(1)} %pad_maximum_fusion.2), channel_id=1, source_target_pairs={{0,8},{1,9},{2,10},{3,11},{4,12},{5,13},{6,14},{7,15},{8,0},{9,1},... | collective-permute-start | bytes 552968 | tf_op jit(solution)/shard_map/ppermute | solution.py:107
  19.0 16.8 %collective-permute-start.3 = (bf16[288,1152]{1,0:T(8,128)(2,1)}, bf16[288,1152]{1,0:T(8,128)(2,1)S(1)}, u32[]{:S(2)}, u32[]{:S(2)}) collective-permute-start(bf16[288,1152]{1,0:T(8,128)(2,1)} %get-tuple-element.20), channel_id=1, source_target_pairs={{0,1},{1,0},{2,3},{3,2},{4,5},{5,4},{6,7},{7,6},{8,9},{9,8},{10,11... | collective-permute-start | bytes 1990664 | tf_op jit(solution)/shard_map/ppermute | solution.py:107
  19.5 20.7 %copy-start.1 = (bf16[20,1152]{1,0:T(8,128)(2,1)S(1)}, bf16[20,1152]{1,0:T(8,128)(2,1)}, u32[]{:S(2)}) copy-start(bf16[20,1152]{1,0:T(8,128)(2,1)} %image.3) | copy-start | bytes 138244
  19.5 6.4 %collective-permute-start.5 = (bf16[88,1152]{1,0:T(8,128)(2,1)S(1)}, bf16[88,1152]{1,0:T(8,128)(2,1)S(1)}, u32[]{:S(2)}, u32[]{:S(2)}) collective-permute-start(bf16[88,1152]{1,0:T(8,128)(2,1)S(1)} %concatenate.16), channel_id=1, source_target_pairs={{0,4},{1,5},{2,6},{3,7},{4,0},{5,1},{6,2},{7,3},{8,12},{9,13},{10,... | collective-permute-start | bytes 608264 | tf_op jit(solution)/shard_map/ppermute | solution.py:107
  26.0 9.7 %collective-permute-start.6 = (bf16[160,1152]{1,0:T(8,128)(2,1)S(1)}, bf16[160,1152]{1,0:T(8,128)(2,1)S(1)}, u32[]{:S(2)}, u32[]{:S(2)}) collective-permute-start(bf16[160,1152]{1,0:T(8,128)(2,1)S(1)} %pad_maximum_fusion.1.rest_0_.rest_2_), channel_id=1, source_target_pairs={{0,2},{1,3},{2,0},{3,1},{4,6},{5,7},{6,4},{7,5},{8,10},{9,11},{10,... | collective-permute-start | bytes 1105928 | tf_op jit(solution)/shard_map/ppermute | solution.py:107
  26.1 11.4 %collective-permute-start.10 = (bf16[168,1152]{1,0:T(8,128)(2,1)S(1)}, bf16[168,1152]{1,0:T(8,128)(2,1)S(1)}, u32[]{:S(2)}, u32[]{:S(2)}) collective-permute-start(bf16[168,1152]{1,0:T(8,128)(2,1)S(1)} %pad_maximum_fusion.rest_6_), channel_id=1, source_target_pairs={{0,8},{1,9},{2,10},{3,11},{4,12},{5,13},{6,14},{7,15},{8,0},{9,1},... | collective-permute-start | bytes 1161224 | tf_op jit(solution)/shard_map/ppermute | solution.py:107
  26.8 10.7 %collective-permute-start.8 = (bf16[160,1152]{1,0:T(8,128)(2,1)S(1)}, bf16[160,1152]{1,0:T(8,128)(2,1)S(1)}, u32[]{:S(2)}, u32[]{:S(2)}) collective-permute-start(bf16[160,1152]{1,0:T(8,128)(2,1)S(1)} %pad_maximum_fusion.1.rest_0_.rest_2_), channel_id=1, source_target_pairs={{0,4},{1,5},{2,6},{3,7},{4,0},{5,1},{6,2},{7,3},{8,12},{9,13},{10,... | collective-permute-start | bytes 1105928 | tf_op jit(solution)/shard_map/ppermute | solution.py:107
  35.7 2.3 %collective-permute-start.7 = (bf16[288,1152]{1,0:T(8,128)(2,1)S(1)}, bf16[288,1152]{1,0:T(8,128)(2,1)S(1)}, u32[]{:S(2)}, u32[]{:S(2)}) collective-permute-start(bf16[288,1152]{1,0:T(8,128)(2,1)S(1)} %collective-permute-done.3.matrix_near), channel_id=1, source_target_pairs={{0,2},{1,3},{2,0},{3,1},{4,6},{5,7},{6,4},{7,5},{8,10},{9,11},{10,... | collective-permute-start | bytes 1990664 | tf_op jit(solution)/shard_map/ppermute | solution.py:107
  35.7 4.4 %collective-permute-start.11 = (bf16[168,1152]{1,0:T(8,128)(2,1)S(1)}, bf16[168,1152]{1,0:T(8,128)(2,1)S(1)}, u32[]{:S(2)}, u32[]{:S(2)}) collective-permute-start(bf16[168,1152]{1,0:T(8,128)(2,1)S(1)} %pad_maximum_fusion.rest_6_), channel_id=1, source_target_pairs={{0,2},{1,3},{2,0},{3,1},{4,6},{5,7},{6,4},{7,5},{8,10},{9,11},{10,... | collective-permute-start | bytes 1161224 | tf_op jit(solution)/shard_map/ppermute | solution.py:107
  37.5 2.7 %collective-permute-start.12 = (bf16[168,1152]{1,0:T(8,128)(2,1)S(1)}, bf16[168,1152]{1,0:T(8,128)(2,1)S(1)}, u32[]{:S(2)}, u32[]{:S(2)}) collective-permute-start(bf16[168,1152]{1,0:T(8,128)(2,1)S(1)} %collective-permute-done.10.rest_7_), channel_id=1, source_target_pairs={{0,2},{1,3},{2,0},{3,1},{4,6},{5,7},{6,4},{7,5},{8,10},{9,11},{10,... | collective-permute-start | bytes 1161224 | tf_op jit(solution)/shard_map/ppermute | solution.py:107
  37.5 2.7 %collective-permute-start.9 = (bf16[160,1152]{1,0:T(8,128)(2,1)S(1)}, bf16[160,1152]{1,0:T(8,128)(2,1)S(1)}, u32[]{:S(2)}, u32[]{:S(2)}) collective-permute-start(bf16[160,1152]{1,0:T(8,128)(2,1)S(1)} %collective-permute-done.8.rest_4_), channel_id=1, source_target_pairs={{0,2},{1,3},{2,0},{3,1},{4,6},{5,7},{6,4},{7,5},{8,10},{9,11},{10,... | collective-permute-start | bytes 1105928 | tf_op jit(solution)/shard_map/ppermute | solution.py:107

commit v2 on v1

--- a/solution.py
+++ b/solution.py
@@ -138,17 +138,13 @@
     return (jnp.where(paired, -sharpness, sharpness) * share).astype(jnp.bfloat16)
 
 
-def own_kernel(image, text, matrix, match, own, plain, quarter, *rest):
-    images, texts, indices, digits, sems = rest
+def own_kernel(image, text, match, own, plain, images, texts, indices, digits, sems):
     rows = images.shape[0]
-    count = quarter.shape[0]
-    start = pl.multiple_of(lax.rem(lax.axis_index("dp"), 2) * count, 32)
     pairs = ((image, images), (text, texts), (match, indices))
-    pairs += ((matrix.at[pl.ds(start, count)], quarter),)
     copies = [pltpu.make_async_copy(*pair, sems.at[k]) for k, pair in enumerate(pairs)]
     for copy in copies:
         copy.start()
-    for copy in copies[:3]:
+    for copy in copies:
         copy.wait()
     width = indices.shape[1]
     digits[...] = jnp.zeros(digits.shape, jnp.float32)
@@ -160,7 +156,6 @@
     text_rows = texts[...].astype(jnp.float32)
     own[1] = jnp.concatenate([text_rows, jnp.zeros_like(spare)]).astype(jnp.bfloat16)
     plain[...] = jnp.concatenate([unit_image, text_rows]).astype(jnp.bfloat16)
-    copies[3].wait()
 
 
 def pair_indices(rows, total, pieces, side):
@@ -256,7 +251,7 @@
         )
     copies = []
     head = grad
-    for k, cut in enumerate(cuts(width, 384)):
+    for k, cut in enumerate(cuts(width, 256)):
         head[:depth, cut] = dot(turned[...], proj[:, cut])
         copies.append(
             pltpu.make_async_copy(head.at[:depth, cut], head_grad.at[:, cut], sems.at[k])
@@ -288,33 +283,33 @@
     params = pltpu.CompilerParams(vmem_limit_bytes=24 * 2**20)
 
     hbm = pl.BlockSpec(memory_space=pltpu.HBM)
-    own, plain, quarter = pl.pallas_call(
+    own, plain = pl.pallas_call(
         own_kernel,
         out_shape=(
             jax.ShapeDtypeStruct((2, rows + 4, width), bf16),
             jax.ShapeDtypeStruct((2 * rows, width), bf16),
-            jax.ShapeDtypeStruct((half, width), bf16),
         ),
-        in_specs=[hbm] * 4,
-        out_specs=(vmem, vmem, vmem),
+        in_specs=[hbm] * 3,
+        out_specs=(vmem, vmem),
         scratch_shapes=[
             pltpu.VMEM((rows, width), bf16),
             pltpu.VMEM((rows, width), bf16),
             pltpu.VMEM((1, 2 * rows), jnp.int32),
             pltpu.VMEM((8, width), f32),
-            pltpu.SemaphoreType.DMA((4,)),
+            pltpu.SemaphoreType.DMA((3,)),
         ],
         name="own_block",
     )(
         picture_mean_embeddings,
         caption_tower_summary,
-        caption_mapping_matrix,
         picture_match_index[None, :],
     )
     first = IMAGE_ORDER[1]
     beside = across(own, first)
     blocks = [plain, across(plain, Y), beside, across(plain, first | Y)]
-    near = across(quarter, Y)
+    matrix, plain = lax.optimization_barrier((caption_mapping_matrix, plain))
+    core = lax.axis_index("dp") % 2
+    quarter = lax.dynamic_slice_in_dim(matrix, core * half, half, 0)
     digits = [block[0, rows : rows + 2] for block in (own, beside)]
     digits += [jnp.zeros((4, width), bf16)]
     images = [block[0, :rows] if block is beside else block[:rows] for block in blocks]
@@ -322,7 +317,9 @@
     texts = [block[1, :rows] if block is beside else block[rows:] for block in blocks]
     texts = jnp.concatenate(texts)
     scalars = jnp.concatenate([sharpness_factor, score_shift_term])[None]
-    texts, images, scalars = lax.optimization_barrier((texts, images, scalars))
+    tied = lax.optimization_barrier((texts, images, scalars, quarter))
+    texts, images, scalars, quarter = tied
+    near = across(quarter, Y)
     texts = jnp.concatenate([texts, across(texts, TEXT_ORDER[2])])
     count = 4 * rows
     beside = across(images, IMAGE_ORDER[2])

time: 49.2 us -> 49.5 us (level)
  local copies, waits for them, and re-layouts: 2.27 us -> 3.42 us
  Pallas kernels: 13.1 us -> 12.4 us
    dynamic_slice x0 -> x1, local copies, waits for them, and re-layouts: none -> 1.15 us  [gathered_plan(): quarter = lax.dynamic_slice_in_dim(matrix, core * half, half, 0)]
    pallas_call x1, Pallas kernels: 2.21 us -> 1.66 us  [gathered_plan(): pl.pallas_call(own_kernel, out_shape=(jax.ShapeDtypeStruct((2, rows + 4,...]
  transfers between devices with their start and end apart: 13 -> 13, of which waited for: 7 -> 7; matrix products, arithmetic and copies ran while one was open for 4% -> 6% of each run, Pallas kernels for 4% -> 4%
where the time goes in v2:
time: 49.5 us; the launch traced here: 49.2 us
  waiting for transfers between devices  19.3 us (39%)
  Pallas kernels  12.4 us (25%)
  starting transfers between devices  11.7 us (24%)
  local copies, waits for them, and re-layouts  3.42 us (7%)
  between operations  2.08 us (4%)
    ppermute x13, waiting for transfers between devices, across(): lax.ppermute(block, ('dp', 'fsdp'), [(i, i ^ bits) for i in range(count)])  19.3 us
    ppermute x13, starting transfers between devices, across(): lax.ppermute(block, ('dp', 'fsdp'), [(i, i ^ bits) for i in range(count)])  11.7 us
    pallas_call x1, Pallas kernels, gathered_plan(): pl.pallas_call(batch_kernel, out_shape=(jax.ShapeDtypeStruct((rows, width...  8.57 us
    pallas_call x1, Pallas kernels, gathered_plan(): pl.pallas_call(early_kernel, out_shape=(jax.ShapeDtypeStruct((total // 2,...  2.14 us
    pallas_call x1, Pallas kernels, gathered_plan(): pl.pallas_call(own_kernel, out_shape=(jax.ShapeDtypeStruct((2, rows + 4,...  1.66 us
    dynamic_slice x1, local copies, waits for them, and re-layouts, gathered_plan(): quarter = lax.dynamic_slice_in_dim(matrix, core * half, half, 0)  1.15 us
  transfers between devices with their start and end apart: 13, of which 7 were waited for; matrix products, arithmetic and copies ran while one was open for 6% of the time, Pallas kernels for 4%

profile of v2, /device:TPU:0, one launch (start us, length us, event | category | flops | bytes accessed | tf_op | source)
XLA Modules:
  0.0 49.2 jit_solution(2332419845378285140)
XLA Ops:
  0.6 1.7 %own_block.1 = (bf16[2,24,1152]{2,1,0:T(8,128)(2,1)}, bf16[40,1152]{1,0:T(8,128)(2,1)}) custom-call(bf16[20,1152]{1,0:T(8,128)(2,1)} %image.3, bf16[20,1152]{1,0:T(8,128)(2,1)} %text.1, s32[1,40]{1,0:T(1,128)} %bitcast.11), custom_call_target="tpu_custom_call" | custom-call | tf_op jit(solution)/shard_map/own_block/pallas_call | solution.py:286
  2.3 5.1 %collective-permute-start.2 = (bf16[40,1152]{1,0:T(8,128)(2,1)}, bf16[40,1152]{1,0:T(8,128)(2,1)S(1)}, u32[]{:S(2)}, u32[]{:S(2)}) collective-permute-start(bf16[40,1152]{1,0:T(8,128)(2,1)} %get-tuple-element.18), channel_id=1, source_target_pairs={{0,17},{1,16},{2,19},{3,18},{4,21},{5,20},{6,23},{7,22},{8,25},{9,... | collective-permute-start | bytes 276488 | tf_op jit(solution)/shard_map/ppermute | solution.py:107
  7.4 0.5 %collective-permute-start = (bf16[40,1152]{1,0:T(8,128)(2,1)}, bf16[40,1152]{1,0:T(8,128)(2,1)S(1)}, u32[]{:S(2)}, u32[]{:S(2)}) collective-permute-start(bf16[40,1152]{1,0:T(8,128)(2,1)} %get-tuple-element.18), channel_id=1, source_target_pairs={{0,1},{1,0},{2,3},{3,2},{4,5},{5,4},{6,7},{7,6},{8,9},{9,8},{10,11... | collective-permute-start | bytes 276488 | tf_op jit(solution)/shard_map/ppermute | solution.py:107
  7.9 0.1 collective-permute-start.1
  8.0 0.8 %slice_bitcast_fusion.3 = bf16[2,1152]{1,0:T(2,128)(2,1)S(1)} fusion(bf16[2,24,1152]{2,1,0:T(8,128)(2,1)} %get-tuple-element.19), kind=kLoop, calls=%fused_computation.6 | loop fusion | bytes 9216 | tf_op jit(solution)/shard_map/squeeze | solution.py:313
  8.8 0.9 %fusion.2 = (bf16[20,1152]{1,0:T(8,128)(2,1)S(1)}, bf16[20,1152]{1,0:T(8,128)(2,1)S(1)}) fusion(bf16[40,1152]{1,0:T(8,128)(2,1)} %get-tuple-element.18), kind=kLoop, calls=%fused_computation.11 | loop fusion | bytes 184320 | tf_op jit(solution)/shard_map/slice | solution.py:315
  11.0 1.1 %constant_dynamic-slice_fusion = bf16[288,1152]{1,0:T(8,128)(2,1)S(1)} fusion(bf16[576,1152]{1,0:T(8,128)(2,1)} %matrix_own.1, s32[]{:T(128)S(6)} %select_n.11), kind=kLoop, calls=%fused_computation.8 | loop fusion | bytes 1327108 | tf_op jit(solution)/shard_map/dynamic_slice | solution.py:312
  12.1 0.1 maximum_bitcast_fusion.scalars
  12.2 0.3 collective-permute-done.2
  12.6 0.4 collective-permute-done
  13.0 4.1 %collective-permute-done.1 = bf16[2,24,1152]{2,1,0:T(8,128)(2,1)S(1)} collective-permute-done((bf16[2,24,1152]{2,1,0:T(8,128)(2,1)}, bf16[2,24,1152]{2,1,0:T(8,128)(2,1)S(1)}, u32[]{:S(2)}, u32[]{:S(2)}) %collective-permute-start.1) | collective-permute-done | bytes 110624 | tf_op jit(solution)/shard_map/ppermute | solution.py:107
  17.1 0.0 copy-start
  17.1 0.5 concatenate.16
  17.6 0.8 %collective-permute-start.4 = (bf16[80,1152]{1,0:T(8,128)(2,1)S(1)}, bf16[80,1152]{1,0:T(8,128)(2,1)S(1)}, u32[]{:S(2)}, u32[]{:S(2)}) collective-permute-start(bf16[80,1152]{1,0:T(8,128)(2,1)S(1)} %pad_maximum_fusion.2), channel_id=1, source_target_pairs={{0,8},{1,9},{2,10},{3,11},{4,12},{5,13},{6,14},{7,15},{8,0},{9,1},... | collective-permute-start | bytes 552968 | tf_op jit(solution)/shard_map/ppermute | solution.py:107
  18.5 1.6 %collective-permute-start.5 = (bf16[88,1152]{1,0:T(8,128)(2,1)S(1)}, bf16[88,1152]{1,0:T(8,128)(2,1)S(1)}, u32[]{:S(2)}, u32[]{:S(2)}) collective-permute-start(bf16[88,1152]{1,0:T(8,128)(2,1)S(1)} %concatenate.16), channel_id=1, source_target_pairs={{0,4},{1,5},{2,6},{3,7},{4,0},{5,1},{6,2},{7,3},{8,12},{9,13},{10,... | collective-permute-start | bytes 608264 | tf_op jit(solution)/shard_map/ppermute | solution.py:107
  20.0 0.5 %collective-permute-start.3 = (bf16[288,1152]{1,0:T(8,128)(2,1)S(1)}, bf16[288,1152]{1,0:T(8,128)(2,1)S(1)}, u32[]{:S(2)}, u32[]{:S(2)}) collective-permute-start(bf16[288,1152]{1,0:T(8,128)(2,1)S(1)} %constant_dynamic-slice_fusion), channel_id=1, source_target_pairs={{0,1},{1,0},{2,3},{3,2},{4,5},{5,4},{6,7},{7,6},{8,9},{9,8},{10,11... | collective-permute-start | bytes 1990664 | tf_op jit(solution)/shard_map/ppermute | solution.py:107
  20.5 3.0 %collective-permute-done.4 = bf16[80,1152]{1,0:T(8,128)(2,1)S(1)} collective-permute-done((bf16[80,1152]{1,0:T(8,128)(2,1)S(1)}, bf16[80,1152]{1,0:T(8,128)(2,1)S(1)}, u32[]{:S(2)}, u32[]{:S(2)}) %collective-permute-start.4) | collective-permute-done | bytes 184352 | tf_op jit(solution)/shard_map/ppermute | solution.py:107
  23.5 1.7 %collective-permute-done.5 = bf16[88,1152]{1,0:T(8,128)(2,1)S(1)} collective-permute-done((bf16[88,1152]{1,0:T(8,128)(2,1)S(1)}, bf16[88,1152]{1,0:T(8,128)(2,1)S(1)}, u32[]{:S(2)}, u32[]{:S(2)}) %collective-permute-start.5) | collective-permute-done | bytes 202784 | tf_op jit(solution)/shard_map/ppermute | solution.py:107
  25.3 0.0 copy-start.1
  25.3 0.1 collective-permute-start.6
  25.4 0.6 %collective-permute-start.10 = (bf16[168,1152]{1,0:T(8,128)(2,1)S(1)}, bf16[168,1152]{1,0:T(8,128)(2,1)S(1)}, u32[]{:S(2)}, u32[]{:S(2)}) collective-permute-start(bf16[168,1152]{1,0:T(8,128)(2,1)S(1)} %pad_maximum_fusion.rest_6_), channel_id=1, source_target_pairs={{0,8},{1,9},{2,10},{3,11},{4,12},{5,13},{6,14},{7,15},{8,0},{9,1},... | collective-permute-start | bytes 1161224 | tf_op jit(solution)/shard_map/ppermute | solution.py:107
  26.0 1.5 %collective-permute-start.8 = (bf16[160,1152]{1,0:T(8,128)(2,1)S(1)}, bf16[160,1152]{1,0:T(8,128)(2,1)S(1)}, u32[]{:S(2)}, u32[]{:S(2)}) collective-permute-start(bf16[160,1152]{1,0:T(8,128)(2,1)S(1)} %pad_maximum_fusion.1.rest_0_.rest_2_), channel_id=1, source_target_pairs={{0,4},{1,5},{2,6},{3,7},{4,0},{5,1},{6,2},{7,3},{8,12},{9,13},{10,... | collective-permute-start | bytes 1105928 | tf_op jit(solution)/shard_map/ppermute | solution.py:107
  27.4 0.0 collective-permute-done.6.rest_1_.rest_3_
  27.4 8.8 %collective-permute-done.3.matrix_near = bf16[288,1152]{1,0:T(8,128)(2,1)S(1)} collective-permute-done((bf16[288,1152]{1,0:T(8,128)(2,1)S(1)}, bf16[288,1152]{1,0:T(8,128)(2,1)S(1)}, u32[]{:S(2)}, u32[]{:S(2)}) %collective-permute-start.3) | collective-permute-done | bytes 663584 | tf_op jit(solution)/shard_map/ppermute | solution.py:107
  36.3 0.0 collective-permute-start.7
  36.3 0.5 %collective-permute-start.11 = (bf16[168,1152]{1,0:T(8,128)(2,1)S(1)}, bf16[168,1152]{1,0:T(8,128)(2,1)S(1)}, u32[]{:S(2)}, u32[]{:S(2)}) collective-permute-start(bf16[168,1152]{1,0:T(8,128)(2,1)S(1)} %pad_maximum_fusion.rest_6_), channel_id=1, source_target_pairs={{0,2},{1,3},{2,0},{3,1},{4,6},{5,7},{6,4},{7,5},{8,10},{9,11},{10,... | collective-permute-start | bytes 1161224 | tf_op jit(solution)/shard_map/ppermute | solution.py:107
  36.8 0.0 collective-permute-done.10.rest_7_
  36.8 0.0 collective-permute-start.12
  36.8 0.0 collective-permute-done.8.rest_4_
  36.8 0.5 %collective-permute-start.9 = (bf16[160,1152]{1,0:T(8,128)(2,1)S(1)}, bf16[160,1152]{1,0:T(8,128)(2,1)S(1)}, u32[]{:S(2)}, u32[]{:S(2)}) collective-permute-start(bf16[160,1152]{1,0:T(8,128)(2,1)S(1)} %collective-permute-done.8.rest_4_), channel_id=1, source_target_pairs={{0,2},{1,3},{2,0},{3,1},{4,6},{5,7},{6,4},{7,5},{8,10},{9,11},{10,... | collective-permute-start | bytes 1105928 | tf_op jit(solution)/shard_map/ppermute | solution.py:107
  37.3 1.1 %collective-permute-done.7.matrix_far = bf16[288,1152]{1,0:T(8,128)(2,1)S(1)} collective-permute-done((bf16[288,1152]{1,0:T(8,128)(2,1)S(1)}, bf16[288,1152]{1,0:T(8,128)(2,1)S(1)}, u32[]{:S(2)}, u32[]{:S(2)}) %collective-permute-start.7) | collective-permute-done | bytes 663584 | tf_op jit(solution)/shard_map/ppermute | solution.py:107
  38.4 0.0 copy-done
  38.4 2.1 %early_texts.1 = (bf16[320,1152]{1,0:T(8,128)(2,1)S(1)}, f32[320,1152]{1,0:T(8,128)S(1)}, bf16[576,256]{1,0:T(8,128)(2,1)S(1)}, bf16[1152,1152]{1,0:T(8,128)(2,1)S(1)}) custom-call(bf16[576,1152]{1,0:T(8,128)(2,1)S(1)} %copy-done, bf16[288,1152]{1,0:T(8,128)(2,1)S(1)} %collective-permute-done.3.matrix_near, ...), custom_call_target="tpu_custom_call" | custom-call | tf_op jit(solution)/shard_map/early_texts/pallas_call | solution.py:333
  40.5 0.0 collective-permute-done.11.rest_8_
  40.6 0.0 collective-permute-done.9.rest_5_
  40.6 0.0 collective-permute-done.12.rest_9_
  40.6 0.0 copy-done.1
  40.6 8.6 %batch.1 = (f32[20,1152]{1,0:T(8,128)}, f32[20,1152]{1,0:T(8,128)}, f32[576,1152]{1,0:T(8,128)}) custom-call(f32[1,2]{1,0:T(1,128)S(1)} %maximum_bitcast_fusion.scalars, bf16[20,1152]{1,0:T(8,128)(2,1)S(1)} %copy-done.1, bf16[320,1152]{1,0:T(8,128)(2,1)S(1)} %get-tuple-element.28.zt_early, f32[320,1152]{1,0:T(8,128)S(1)} %get-tuple-element.29.projected_early, ...), custom_call_target="tpu_custom_call" | custom-call | tf_op jit(solution)/shard_map/batch/pallas_call | solution.py:349
  (12 shorter events, 0.2 us)
Async XLA Ops:
  2.3 10.2 %collective-permute-start.2 = (bf16[40,1152]{1,0:T(8,128)(2,1)}, bf16[40,1152]{1,0:T(8,128)(2,1)S(1)}, u32[]{:S(2)}, u32[]{:S(2)}) collective-permute-start(bf16[40,1152]{1,0:T(8,128)(2,1)} %get-tuple-element.18), channel_id=1, source_target_pairs={{0,17},{1,16},{2,19},{3,18},{4,21},{5,20},{6,23},{7,22},{8,25},{9,... | collective-permute-start | bytes 276488 | tf_op jit(solution)/shard_map/ppermute | solution.py:107
  7.4 5.6 %collective-permute-start = (bf16[40,1152]{1,0:T(8,128)(2,1)}, bf16[40,1152]{1,0:T(8,128)(2,1)S(1)}, u32[]{:S(2)}, u32[]{:S(2)}) collective-permute-start(bf16[40,1152]{1,0:T(8,128)(2,1)} %get-tuple-element.18), channel_id=1, source_target_pairs={{0,1},{1,0},{2,3},{3,2},{4,5},{5,4},{6,7},{7,6},{8,9},{9,8},{10,11... | collective-permute-start | bytes 276488 | tf_op jit(solution)/shard_map/ppermute | solution.py:107
  7.9 9.2 %collective-permute-start.1 = (bf16[2,24,1152]{2,1,0:T(8,128)(2,1)}, bf16[2,24,1152]{2,1,0:T(8,128)(2,1)S(1)}, u32[]{:S(2)}, u32[]{:S(2)}) collective-permute-start(bf16[2,24,1152]{2,1,0:T(8,128)(2,1)} %get-tuple-element.19), channel_id=1, source_target_pairs={{0,16},{1,17},{2,18},{3,19},{4,20},{5,21},{6,22},{7,23},{8,24},{9,... | collective-permute-start | bytes 331784 | tf_op jit(solution)/shard_map/ppermute | solution.py:107
  17.1 21.3 %copy-start = (bf16[576,1152]{1,0:T(8,128)(2,1)S(1)}, bf16[576,1152]{1,0:T(8,128)(2,1)}, u32[]{:S(2)}) copy-start(bf16[576,1152]{1,0:T(8,128)(2,1)} %matrix_own.1) | copy-start | bytes 3981316
  17.6 5.9 %collective-permute-start.4 = (bf16[80,1152]{1,0:T(8,128)(2,1)S(1)}, bf16[80,1152]{1,0:T(8,128)(2,1)S(1)}, u32[]{:S(2)}, u32[]{:S(2)}) collective-permute-start(bf16[80,1152]{1,0:T(8,128)(2,1)S(1)} %pad_maximum_fusion.2), channel_id=1, source_target_pairs={{0,8},{1,9},{2,10},{3,11},{4,12},{5,13},{6,14},{7,15},{8,0},{9,1},... | collective-permute-start | bytes 552968 | tf_op jit(solution)/shard_map/ppermute | solution.py:107
  18.5 6.7 %collective-permute-start.5 = (bf16[88,1152]{1,0:T(8,128)(2,1)S(1)}, bf16[88,1152]{1,0:T(8,128)(2,1)S(1)}, u32[]{:S(2)}, u32[]{:S(2)}) collective-permute-start(bf16[88,1152]{1,0:T(8,128)(2,1)S(1)} %concatenate.16), channel_id=1, source_target_pairs={{0,4},{1,5},{2,6},{3,7},{4,0},{5,1},{6,2},{7,3},{8,12},{9,13},{10,... | collective-permute-start | bytes 608264 | tf_op jit(solution)/shard_map/ppermute | solution.py:107
  20.0 16.3 %collective-permute-start.3 = (bf16[288,1152]{1,0:T(8,128)(2,1)S(1)}, bf16[288,1152]{1,0:T(8,128)(2,1)S(1)}, u32[]{:S(2)}, u32[]{:S(2)}) collective-permute-start(bf16[288,1152]{1,0:T(8,128)(2,1)S(1)} %constant_dynamic-slice_fusion), channel_id=1, source_target_pairs={{0,1},{1,0},{2,3},{3,2},{4,5},{5,4},{6,7},{7,6},{8,9},{9,8},{10,11... | collective-permute-start | bytes 1990664 | tf_op jit(solution)/shard_map/ppermute | solution.py:107
  25.3 15.3 %copy-start.1 = (bf16[20,1152]{1,0:T(8,128)(2,1)S(1)}, bf16[20,1152]{1,0:T(8,128)(2,1)}, u32[]{:S(2)}) copy-start(bf16[20,1152]{1,0:T(8,128)(2,1)} %image.3) | copy-start | bytes 138244
  25.3 2.2 %collective-permute-start.6 = (bf16[160,1152]{1,0:T(8,128)(2,1)S(1)}, bf16[160,1152]{1,0:T(8,128)(2,1)S(1)}, u32[]{:S(2)}, u32[]{:S(2)}) collective-permute-start(bf16[160,1152]{1,0:T(8,128)(2,1)S(1)} %pad_maximum_fusion.1.rest_0_.rest_2_), channel_id=1, source_target_pairs={{0,2},{1,3},{2,0},{3,1},{4,6},{5,7},{6,4},{7,5},{8,10},{9,11},{10,... | collective-permute-start | bytes 1105928 | tf_op jit(solution)/shard_map/ppermute | solution.py:107
  25.4 11.4 %collective-permute-start.10 = (bf16[168,1152]{1,0:T(8,128)(2,1)S(1)}, bf16[168,1152]{1,0:T(8,128)(2,1)S(1)}, u32[]{:S(2)}, u32[]{:S(2)}) collective-permute-start(bf16[168,1152]{1,0:T(8,128)(2,1)S(1)} %pad_maximum_fusion.rest_6_), channel_id=1, source_target_pairs={{0,8},{1,9},{2,10},{3,11},{4,12},{5,13},{6,14},{7,15},{8,0},{9,1},... | collective-permute-start | bytes 1161224 | tf_op jit(solution)/shard_map/ppermute | solution.py:107
  26.0 10.9 %collective-permute-start.8 = (bf16[160,1152]{1,0:T(8,128)(2,1)S(1)}, bf16[160,1152]{1,0:T(8,128)(2,1)S(1)}, u32[]{:S(2)}, u32[]{:S(2)}) collective-permute-start(bf16[160,1152]{1,0:T(8,128)(2,1)S(1)} %pad_maximum_fusion.1.rest_0_.rest_2_), channel_id=1, source_target_pairs={{0,4},{1,5},{2,6},{3,7},{4,0},{5,1},{6,2},{7,3},{8,12},{9,13},{10,... | collective-permute-start | bytes 1105928 | tf_op jit(solution)/shard_map/ppermute | solution.py:107
  36.3 2.1 %collective-permute-start.7 = (bf16[288,1152]{1,0:T(8,128)(2,1)S(1)}, bf16[288,1152]{1,0:T(8,128)(2,1)S(1)}, u32[]{:S(2)}, u32[]{:S(2)}) collective-permute-start(bf16[288,1152]{1,0:T(8,128)(2,1)S(1)} %collective-permute-done.3.matrix_near), channel_id=1, source_target_pairs={{0,2},{1,3},{2,0},{3,1},{4,6},{5,7},{6,4},{7,5},{8,10},{9,11},{10,... | collective-permute-start | bytes 1990664 | tf_op jit(solution)/shard_map/ppermute | solution.py:107
  36.3 4.3 %collective-permute-start.11 = (bf16[168,1152]{1,0:T(8,128)(2,1)S(1)}, bf16[168,1152]{1,0:T(8,128)(2,1)S(1)}, u32[]{:S(2)}, u32[]{:S(2)}) collective-permute-start(bf16[168,1152]{1,0:T(8,128)(2,1)S(1)} %pad_maximum_fusion.rest_6_), channel_id=1, source_target_pairs={{0,2},{1,3},{2,0},{3,1},{4,6},{5,7},{6,4},{7,5},{8,10},{9,11},{10,... | collective-permute-start | bytes 1161224 | tf_op jit(solution)/shard_map/ppermute | solution.py:107
  36.8 3.8 %collective-permute-start.12 = (bf16[168,1152]{1,0:T(8,128)(2,1)S(1)}, bf16[168,1152]{1,0:T(8,128)(2,1)S(1)}, u32[]{:S(2)}, u32[]{:S(2)}) collective-permute-start(bf16[168,1152]{1,0:T(8,128)(2,1)S(1)} %collective-permute-done.10.rest_7_), channel_id=1, source_target_pairs={{0,2},{1,3},{2,0},{3,1},{4,6},{5,7},{6,4},{7,5},{8,10},{9,11},{10,... | collective-permute-start | bytes 1161224 | tf_op jit(solution)/shard_map/ppermute | solution.py:107
  36.8 3.8 %collective-permute-start.9 = (bf16[160,1152]{1,0:T(8,128)(2,1)S(1)}, bf16[160,1152]{1,0:T(8,128)(2,1)S(1)}, u32[]{:S(2)}, u32[]{:S(2)}) collective-permute-start(bf16[160,1152]{1,0:T(8,128)(2,1)S(1)} %collective-permute-done.8.rest_4_), channel_id=1, source_target_pairs={{0,2},{1,3},{2,0},{3,1},{4,6},{5,7},{6,4},{7,5},{8,10},{9,11},{10,... | collective-permute-start | bytes 1105928 | tf_op jit(solution)/shard_map/ppermute | solution.py:107

commit v3 on v2

--- a/solution.py
+++ b/solution.py
@@ -138,28 +138,21 @@
     return (jnp.where(paired, -sharpness, sharpness) * share).astype(jnp.bfloat16)
 
 
-def own_kernel(image, text, match, own, plain, images, texts, indices, digits, sems):
-    rows = images.shape[0]
-    pairs = ((image, images), (text, texts), (match, indices))
-    copies = [pltpu.make_async_copy(*pair, sems.at[k]) for k, pair in enumerate(pairs)]
-    for copy in copies:
-        copy.start()
-    for copy in copies:
-        copy.wait()
-    width = indices.shape[1]
+def own_kernel(image, text, match, own, plain, digits):
+    rows, width = image.shape[0], match.shape[1]
     digits[...] = jnp.zeros(digits.shape, jnp.float32)
-    digits[0:1, :width] = (indices[...] >> 5).astype(jnp.float32)
-    digits[1:2, :width] = (indices[...] & 31).astype(jnp.float32)
+    digits[0:1, :width] = (match[...] >> 5).astype(jnp.float32)
+    digits[1:2, :width] = (match[...] & 31).astype(jnp.float32)
     spare = digits[: own.shape[1] - rows]
-    unit_image, _ = normalize(images[...].astype(jnp.float32))
+    unit_image, _ = normalize(image[...].astype(jnp.float32))
     own[0] = jnp.concatenate([unit_image, spare]).astype(jnp.bfloat16)
-    text_rows = texts[...].astype(jnp.float32)
+    text_rows = text[...].astype(jnp.float32)
     own[1] = jnp.concatenate([text_rows, jnp.zeros_like(spare)]).astype(jnp.bfloat16)
     plain[...] = jnp.concatenate([unit_image, text_rows]).astype(jnp.bfloat16)
 
 
 def pair_indices(rows, total, pieces, side):
-    digits = jnp.concatenate([piece[-8:, :128].astype(jnp.float32) for piece in pieces])
+    digits = jnp.concatenate([piece[...].astype(jnp.float32)[-8:, :128] for piece in pieces])
     lane = lax.broadcasted_iota(jnp.int32, (1, total), 1)
     group = sum((lane >= k).astype(jnp.int32) for k in range(2 * rows, total, 2 * rows))
     row = lane - group * 2 * rows
@@ -282,22 +275,15 @@
     f32, bf16 = jnp.float32, jnp.bfloat16
     params = pltpu.CompilerParams(vmem_limit_bytes=24 * 2**20)
 
-    hbm = pl.BlockSpec(memory_space=pltpu.HBM)
     own, plain = pl.pallas_call(
         own_kernel,
         out_shape=(
             jax.ShapeDtypeStruct((2, rows + 4, width), bf16),
             jax.ShapeDtypeStruct((2 * rows, width), bf16),
         ),
-        in_specs=[hbm] * 3,
+        in_specs=[vmem] * 3,
         out_specs=(vmem, vmem),
-        scratch_shapes=[
-            pltpu.VMEM((rows, width), bf16),
-            pltpu.VMEM((rows, width), bf16),
-            pltpu.VMEM((1, 2 * rows), jnp.int32),
-            pltpu.VMEM((8, width), f32),
-            pltpu.SemaphoreType.DMA((3,)),
-        ],
+        scratch_shapes=[pltpu.VMEM((8, width), f32)],
         name="own_block",
     )(
         picture_mean_embeddings,

time: 49.5 us -> 49.4 us (level)
  no operation moved by 1% of the time
where the time goes in v3:
time: 49.4 us; the launch traced here: 49.1 us
  waiting for transfers between devices  19.4 us (39%)
  Pallas kernels  12.3 us (25%)
  starting transfers between devices  11.6 us (23%)
  local copies, waits for them, and re-layouts  3.42 us (7%)
  between operations  2.08 us (4%)
    ppermute x13, waiting for transfers between devices, across(): lax.ppermute(block, ('dp', 'fsdp'), [(i, i ^ bits) for i in range(count)])  19.4 us
    ppermute x13, starting transfers between devices, across(): lax.ppermute(block, ('dp', 'fsdp'), [(i, i ^ bits) for i in range(count)])  11.6 us
    pallas_call x1, Pallas kernels, gathered_plan(): pl.pallas_call(batch_kernel, out_shape=(jax.ShapeDtypeStruct((rows, width...  8.57 us
    pallas_call x1, Pallas kernels, gathered_plan(): pl.pallas_call(early_kernel, out_shape=(jax.ShapeDtypeStruct((total // 2,...  2.14 us
    pallas_call x1, Pallas kernels, gathered_plan(): pl.pallas_call(own_kernel, out_shape=(jax.ShapeDtypeStruct((2, rows + 4,...  1.63 us
    dynamic_slice x1, local copies, waits for them, and re-layouts, gathered_plan(): quarter = lax.dynamic_slice_in_dim(matrix, core * half, half, 0)  1.15 us
  transfers between devices with their start and end apart: 13, of which 7 were waited for; matrix products, arithmetic and copies ran while one was open for 6% of the time, Pallas kernels for 4%

profile of v3, /device:TPU:0, one launch (start us, length us, event | category | flops | bytes accessed | tf_op | source)
XLA Modules:
  0.0 49.1 jit_solution(5594000472300327617)
XLA Ops:
  0.6 1.6 %own_block.1 = (bf16[2,24,1152]{2,1,0:T(8,128)(2,1)}, bf16[40,1152]{1,0:T(8,128)(2,1)}) custom-call(bf16[20,1152]{1,0:T(8,128)(2,1)} %image.3, bf16[20,1152]{1,0:T(8,128)(2,1)} %text.1, s32[1,40]{1,0:T(1,128)} %bitcast.11), custom_call_target="tpu_custom_call" | custom-call | tf_op jit(solution)/shard_map/own_block/pallas_call | solution.py:278
  2.3 5.0 %collective-permute-start.2 = (bf16[40,1152]{1,0:T(8,128)(2,1)}, bf16[40,1152]{1,0:T(8,128)(2,1)S(1)}, u32[]{:S(2)}, u32[]{:S(2)}) collective-permute-start(bf16[40,1152]{1,0:T(8,128)(2,1)} %get-tuple-element.18), channel_id=1, source_target_pairs={{0,17},{1,16},{2,19},{3,18},{4,21},{5,20},{6,23},{7,22},{8,25},{9,... | collective-permute-start | bytes 276488 | tf_op jit(solution)/shard_map/ppermute | solution.py:107
  7.3 0.5 %collective-permute-start = (bf16[40,1152]{1,0:T(8,128)(2,1)}, bf16[40,1152]{1,0:T(8,128)(2,1)S(1)}, u32[]{:S(2)}, u32[]{:S(2)}) collective-permute-start(bf16[40,1152]{1,0:T(8,128)(2,1)} %get-tuple-element.18), channel_id=1, source_target_pairs={{0,1},{1,0},{2,3},{3,2},{4,5},{5,4},{6,7},{7,6},{8,9},{9,8},{10,11... | collective-permute-start | bytes 276488 | tf_op jit(solution)/shard_map/ppermute | solution.py:107
  7.8 0.1 collective-permute-start.1
  7.8 0.8 %slice_bitcast_fusion.3 = bf16[2,1152]{1,0:T(2,128)(2,1)S(1)} fusion(bf16[2,24,1152]{2,1,0:T(8,128)(2,1)} %get-tuple-element.19), kind=kLoop, calls=%fused_computation.6 | loop fusion | bytes 9216 | tf_op jit(solution)/shard_map/squeeze | solution.py:299
  8.6 0.9 %fusion.2 = (bf16[20,1152]{1,0:T(8,128)(2,1)S(1)}, bf16[20,1152]{1,0:T(8,128)(2,1)S(1)}) fusion(bf16[40,1152]{1,0:T(8,128)(2,1)} %get-tuple-element.18), kind=kLoop, calls=%fused_computation.11 | loop fusion | bytes 184320 | tf_op jit(solution)/shard_map/slice | solution.py:301
  10.8 1.1 %constant_dynamic-slice_fusion = bf16[288,1152]{1,0:T(8,128)(2,1)S(1)} fusion(bf16[576,1152]{1,0:T(8,128)(2,1)} %matrix_own.1, s32[]{:T(128)S(6)} %select_n.11), kind=kLoop, calls=%fused_computation.8 | loop fusion | bytes 1327108 | tf_op jit(solution)/shard_map/dynamic_slice | solution.py:298
  12.0 0.1 maximum_bitcast_fusion.scalars
  12.0 0.4 collective-permute-done.2
  12.5 0.4 collective-permute-done
  12.9 4.1 %collective-permute-done.1 = bf16[2,24,1152]{2,1,0:T(8,128)(2,1)S(1)} collective-permute-done((bf16[2,24,1152]{2,1,0:T(8,128)(2,1)}, bf16[2,24,1152]{2,1,0:T(8,128)(2,1)S(1)}, u32[]{:S(2)}, u32[]{:S(2)}) %collective-permute-start.1) | collective-permute-done | bytes 110624 | tf_op jit(solution)/shard_map/ppermute | solution.py:107
  17.0 0.0 copy-start
  17.0 0.5 concatenate.16
  17.5 0.8 %collective-permute-start.4 = (bf16[80,1152]{1,0:T(8,128)(2,1)S(1)}, bf16[80,1152]{1,0:T(8,128)(2,1)S(1)}, u32[]{:S(2)}, u32[]{:S(2)}) collective-permute-start(bf16[80,1152]{1,0:T(8,128)(2,1)S(1)} %pad_maximum_fusion.2), channel_id=1, source_target_pairs={{0,8},{1,9},{2,10},{3,11},{4,12},{5,13},{6,14},{7,15},{8,0},{9,1},... | collective-permute-start | bytes 552968 | tf_op jit(solution)/shard_map/ppermute | solution.py:107
  18.4 1.6 %collective-permute-start.5 = (bf16[88,1152]{1,0:T(8,128)(2,1)S(1)}, bf16[88,1152]{1,0:T(8,128)(2,1)S(1)}, u32[]{:S(2)}, u32[]{:S(2)}) collective-permute-start(bf16[88,1152]{1,0:T(8,128)(2,1)S(1)} %concatenate.16), channel_id=1, source_target_pairs={{0,4},{1,5},{2,6},{3,7},{4,0},{5,1},{6,2},{7,3},{8,12},{9,13},{10,... | collective-permute-start | bytes 608264 | tf_op jit(solution)/shard_map/ppermute | solution.py:107
  19.9 0.5 %collective-permute-start.3 = (bf16[288,1152]{1,0:T(8,128)(2,1)S(1)}, bf16[288,1152]{1,0:T(8,128)(2,1)S(1)}, u32[]{:S(2)}, u32[]{:S(2)}) collective-permute-start(bf16[288,1152]{1,0:T(8,128)(2,1)S(1)} %constant_dynamic-slice_fusion), channel_id=1, source_target_pairs={{0,1},{1,0},{2,3},{3,2},{4,5},{5,4},{6,7},{7,6},{8,9},{9,8},{10,11... | collective-permute-start | bytes 1990664 | tf_op jit(solution)/shard_map/ppermute | solution.py:107
  20.4 3.0 %collective-permute-done.4 = bf16[80,1152]{1,0:T(8,128)(2,1)S(1)} collective-permute-done((bf16[80,1152]{1,0:T(8,128)(2,1)S(1)}, bf16[80,1152]{1,0:T(8,128)(2,1)S(1)}, u32[]{:S(2)}, u32[]{:S(2)}) %collective-permute-start.4) | collective-permute-done | bytes 184352 | tf_op jit(solution)/shard_map/ppermute | solution.py:107
  23.4 1.7 %collective-permute-done.5 = bf16[88,1152]{1,0:T(8,128)(2,1)S(1)} collective-permute-done((bf16[88,1152]{1,0:T(8,128)(2,1)S(1)}, bf16[88,1152]{1,0:T(8,128)(2,1)S(1)}, u32[]{:S(2)}, u32[]{:S(2)}) %collective-permute-start.5) | collective-permute-done | bytes 202784 | tf_op jit(solution)/shard_map/ppermute | solution.py:107
  25.2 0.0 copy-start.1
  25.2 0.1 collective-permute-start.6
  25.3 0.6 %collective-permute-start.10 = (bf16[168,1152]{1,0:T(8,128)(2,1)S(1)}, bf16[168,1152]{1,0:T(8,128)(2,1)S(1)}, u32[]{:S(2)}, u32[]{:S(2)}) collective-permute-start(bf16[168,1152]{1,0:T(8,128)(2,1)S(1)} %pad_maximum_fusion.rest_6_), channel_id=1, source_target_pairs={{0,8},{1,9},{2,10},{3,11},{4,12},{5,13},{6,14},{7,15},{8,0},{9,1},... | collective-permute-start | bytes 1161224 | tf_op jit(solution)/shard_map/ppermute | solution.py:107
  25.9 1.5 %collective-permute-start.8 = (bf16[160,1152]{1,0:T(8,128)(2,1)S(1)}, bf16[160,1152]{1,0:T(8,128)(2,1)S(1)}, u32[]{:S(2)}, u32[]{:S(2)}) collective-permute-start(bf16[160,1152]{1,0:T(8,128)(2,1)S(1)} %pad_maximum_fusion.1.rest_0_.rest_2_), channel_id=1, source_target_pairs={{0,4},{1,5},{2,6},{3,7},{4,0},{5,1},{6,2},{7,3},{8,12},{9,13},{10,... | collective-permute-start | bytes 1105928 | tf_op jit(solution)/shard_map/ppermute | solution.py:107
  27.3 0.0 collective-permute-done.6.rest_1_.rest_3_
  27.3 8.8 %collective-permute-done.3.matrix_near = bf16[288,1152]{1,0:T(8,128)(2,1)S(1)} collective-permute-done((bf16[288,1152]{1,0:T(8,128)(2,1)S(1)}, bf16[288,1152]{1,0:T(8,128)(2,1)S(1)}, u32[]{:S(2)}, u32[]{:S(2)}) %collective-permute-start.3) | collective-permute-done | bytes 663584 | tf_op jit(solution)/shard_map/ppermute | solution.py:107
  36.2 0.0 collective-permute-start.7
  36.2 0.5 %collective-permute-start.11 = (bf16[168,1152]{1,0:T(8,128)(2,1)S(1)}, bf16[168,1152]{1,0:T(8,128)(2,1)S(1)}, u32[]{:S(2)}, u32[]{:S(2)}) collective-permute-start(bf16[168,1152]{1,0:T(8,128)(2,1)S(1)} %pad_maximum_fusion.rest_6_), channel_id=1, source_target_pairs={{0,2},{1,3},{2,0},{3,1},{4,6},{5,7},{6,4},{7,5},{8,10},{9,11},{10,... | collective-permute-start | bytes 1161224 | tf_op jit(solution)/shard_map/ppermute | solution.py:107
  36.7 0.0 collective-permute-done.10.rest_7_
  36.7 0.0 collective-permute-start.12
  36.7 0.0 collective-permute-done.8.rest_4_
  36.7 0.5 %collective-permute-start.9 = (bf16[160,1152]{1,0:T(8,128)(2,1)S(1)}, bf16[160,1152]{1,0:T(8,128)(2,1)S(1)}, u32[]{:S(2)}, u32[]{:S(2)}) collective-permute-start(bf16[160,1152]{1,0:T(8,128)(2,1)S(1)} %collective-permute-done.8.rest_4_), channel_id=1, source_target_pairs={{0,2},{1,3},{2,0},{3,1},{4,6},{5,7},{6,4},{7,5},{8,10},{9,11},{10,... | collective-permute-start | bytes 1105928 | tf_op jit(solution)/shard_map/ppermute | solution.py:107
  37.2 1.1 %collective-permute-done.7.matrix_far = bf16[288,1152]{1,0:T(8,128)(2,1)S(1)} collective-permute-done((bf16[288,1152]{1,0:T(8,128)(2,1)S(1)}, bf16[288,1152]{1,0:T(8,128)(2,1)S(1)}, u32[]{:S(2)}, u32[]{:S(2)}) %collective-permute-start.7) | collective-permute-done | bytes 663584 | tf_op jit(solution)/shard_map/ppermute | solution.py:107
  38.3 0.0 copy-done
  38.3 2.1 %early_texts.1 = (bf16[320,1152]{1,0:T(8,128)(2,1)S(1)}, f32[320,1152]{1,0:T(8,128)S(1)}, bf16[576,256]{1,0:T(8,128)(2,1)S(1)}, bf16[1152,1152]{1,0:T(8,128)(2,1)S(1)}) custom-call(bf16[576,1152]{1,0:T(8,128)(2,1)S(1)} %copy-done, bf16[288,1152]{1,0:T(8,128)(2,1)S(1)} %collective-permute-done.3.matrix_near, ...), custom_call_target="tpu_custom_call" | custom-call | tf_op jit(solution)/shard_map/early_texts/pallas_call | solution.py:319
  40.4 0.0 collective-permute-done.11.rest_8_
  40.5 0.0 collective-permute-done.9.rest_5_
  40.5 0.0 collective-permute-done.12.rest_9_
  40.5 0.0 copy-done.1
  40.5 8.6 %batch.1 = (f32[20,1152]{1,0:T(8,128)}, f32[20,1152]{1,0:T(8,128)}, f32[576,1152]{1,0:T(8,128)}) custom-call(f32[1,2]{1,0:T(1,128)S(1)} %maximum_bitcast_fusion.scalars, bf16[20,1152]{1,0:T(8,128)(2,1)S(1)} %copy-done.1, bf16[320,1152]{1,0:T(8,128)(2,1)S(1)} %get-tuple-element.28.zt_early, f32[320,1152]{1,0:T(8,128)S(1)} %get-tuple-element.29.projected_early, ...), custom_call_target="tpu_custom_call" | custom-call | tf_op jit(solution)/shard_map/batch/pallas_call | solution.py:335
  (12 shorter events, 0.2 us)
Async XLA Ops:
  2.3 10.2 %collective-permute-start.2 = (bf16[40,1152]{1,0:T(8,128)(2,1)}, bf16[40,1152]{1,0:T(8,128)(2,1)S(1)}, u32[]{:S(2)}, u32[]{:S(2)}) collective-permute-start(bf16[40,1152]{1,0:T(8,128)(2,1)} %get-tuple-element.18), channel_id=1, source_target_pairs={{0,17},{1,16},{2,19},{3,18},{4,21},{5,20},{6,23},{7,22},{8,25},{9,... | collective-permute-start | bytes 276488 | tf_op jit(solution)/shard_map/ppermute | solution.py:107
  7.3 5.6 %collective-permute-start = (bf16[40,1152]{1,0:T(8,128)(2,1)}, bf16[40,1152]{1,0:T(8,128)(2,1)S(1)}, u32[]{:S(2)}, u32[]{:S(2)}) collective-permute-start(bf16[40,1152]{1,0:T(8,128)(2,1)} %get-tuple-element.18), channel_id=1, source_target_pairs={{0,1},{1,0},{2,3},{3,2},{4,5},{5,4},{6,7},{7,6},{8,9},{9,8},{10,11... | collective-permute-start | bytes 276488 | tf_op jit(solution)/shard_map/ppermute | solution.py:107
  7.8 9.2 %collective-permute-start.1 = (bf16[2,24,1152]{2,1,0:T(8,128)(2,1)}, bf16[2,24,1152]{2,1,0:T(8,128)(2,1)S(1)}, u32[]{:S(2)}, u32[]{:S(2)}) collective-permute-start(bf16[2,24,1152]{2,1,0:T(8,128)(2,1)} %get-tuple-element.19), channel_id=1, source_target_pairs={{0,16},{1,17},{2,18},{3,19},{4,20},{5,21},{6,22},{7,23},{8,24},{9,... | collective-permute-start | bytes 331784 | tf_op jit(solution)/shard_map/ppermute | solution.py:107
  17.0 21.3 %copy-start = (bf16[576,1152]{1,0:T(8,128)(2,1)S(1)}, bf16[576,1152]{1,0:T(8,128)(2,1)}, u32[]{:S(2)}) copy-start(bf16[576,1152]{1,0:T(8,128)(2,1)} %matrix_own.1) | copy-start | bytes 3981316
  17.5 5.9 %collective-permute-start.4 = (bf16[80,1152]{1,0:T(8,128)(2,1)S(1)}, bf16[80,1152]{1,0:T(8,128)(2,1)S(1)}, u32[]{:S(2)}, u32[]{:S(2)}) collective-permute-start(bf16[80,1152]{1,0:T(8,128)(2,1)S(1)} %pad_maximum_fusion.2), channel_id=1, source_target_pairs={{0,8},{1,9},{2,10},{3,11},{4,12},{5,13},{6,14},{7,15},{8,0},{9,1},... | collective-permute-start | bytes 552968 | tf_op jit(solution)/shard_map/ppermute | solution.py:107
  18.4 6.7 %collective-permute-start.5 = (bf16[88,1152]{1,0:T(8,128)(2,1)S(1)}, bf16[88,1152]{1,0:T(8,128)(2,1)S(1)}, u32[]{:S(2)}, u32[]{:S(2)}) collective-permute-start(bf16[88,1152]{1,0:T(8,128)(2,1)S(1)} %concatenate.16), channel_id=1, source_target_pairs={{0,4},{1,5},{2,6},{3,7},{4,0},{5,1},{6,2},{7,3},{8,12},{9,13},{10,... | collective-permute-start | bytes 608264 | tf_op jit(solution)/shard_map/ppermute | solution.py:107
  19.9 16.3 %collective-permute-start.3 = (bf16[288,1152]{1,0:T(8,128)(2,1)S(1)}, bf16[288,1152]{1,0:T(8,128)(2,1)S(1)}, u32[]{:S(2)}, u32[]{:S(2)}) collective-permute-start(bf16[288,1152]{1,0:T(8,128)(2,1)S(1)} %constant_dynamic-slice_fusion), channel_id=1, source_target_pairs={{0,1},{1,0},{2,3},{3,2},{4,5},{5,4},{6,7},{7,6},{8,9},{9,8},{10,11... | collective-permute-start | bytes 1990664 | tf_op jit(solution)/shard_map/ppermute | solution.py:107
  25.2 15.3 %copy-start.1 = (bf16[20,1152]{1,0:T(8,128)(2,1)S(1)}, bf16[20,1152]{1,0:T(8,128)(2,1)}, u32[]{:S(2)}) copy-start(bf16[20,1152]{1,0:T(8,128)(2,1)} %image.3) | copy-start | bytes 138244
  25.2 2.2 %collective-permute-start.6 = (bf16[160,1152]{1,0:T(8,128)(2,1)S(1)}, bf16[160,1152]{1,0:T(8,128)(2,1)S(1)}, u32[]{:S(2)}, u32[]{:S(2)}) collective-permute-start(bf16[160,1152]{1,0:T(8,128)(2,1)S(1)} %pad_maximum_fusion.1.rest_0_.rest_2_), channel_id=1, source_target_pairs={{0,2},{1,3},{2,0},{3,1},{4,6},{5,7},{6,4},{7,5},{8,10},{9,11},{10,... | collective-permute-start | bytes 1105928 | tf_op jit(solution)/shard_map/ppermute | solution.py:107
  25.3 11.4 %collective-permute-start.10 = (bf16[168,1152]{1,0:T(8,128)(2,1)S(1)}, bf16[168,1152]{1,0:T(8,128)(2,1)S(1)}, u32[]{:S(2)}, u32[]{:S(2)}) collective-permute-start(bf16[168,1152]{1,0:T(8,128)(2,1)S(1)} %pad_maximum_fusion.rest_6_), channel_id=1, source_target_pairs={{0,8},{1,9},{2,10},{3,11},{4,12},{5,13},{6,14},{7,15},{8,0},{9,1},... | collective-permute-start | bytes 1161224 | tf_op jit(solution)/shard_map/ppermute | solution.py:107
  25.9 10.9 %collective-permute-start.8 = (bf16[160,1152]{1,0:T(8,128)(2,1)S(1)}, bf16[160,1152]{1,0:T(8,128)(2,1)S(1)}, u32[]{:S(2)}, u32[]{:S(2)}) collective-permute-start(bf16[160,1152]{1,0:T(8,128)(2,1)S(1)} %pad_maximum_fusion.1.rest_0_.rest_2_), channel_id=1, source_target_pairs={{0,4},{1,5},{2,6},{3,7},{4,0},{5,1},{6,2},{7,3},{8,12},{9,13},{10,... | collective-permute-start | bytes 1105928 | tf_op jit(solution)/shard_map/ppermute | solution.py:107
  36.2 2.1 %collective-permute-start.7 = (bf16[288,1152]{1,0:T(8,128)(2,1)S(1)}, bf16[288,1152]{1,0:T(8,128)(2,1)S(1)}, u32[]{:S(2)}, u32[]{:S(2)}) collective-permute-start(bf16[288,1152]{1,0:T(8,128)(2,1)S(1)} %collective-permute-done.3.matrix_near), channel_id=1, source_target_pairs={{0,2},{1,3},{2,0},{3,1},{4,6},{5,7},{6,4},{7,5},{8,10},{9,11},{10,... | collective-permute-start | bytes 1990664 | tf_op jit(solution)/shard_map/ppermute | solution.py:107
  36.2 4.3 %collective-permute-start.11 = (bf16[168,1152]{1,0:T(8,128)(2,1)S(1)}, bf16[168,1152]{1,0:T(8,128)(2,1)S(1)}, u32[]{:S(2)}, u32[]{:S(2)}) collective-permute-start(bf16[168,1152]{1,0:T(8,128)(2,1)S(1)} %pad_maximum_fusion.rest_6_), channel_id=1, source_target_pairs={{0,2},{1,3},{2,0},{3,1},{4,6},{5,7},{6,4},{7,5},{8,10},{9,11},{10,... | collective-permute-start | bytes 1161224 | tf_op jit(solution)/shard_map/ppermute | solution.py:107
  36.7 3.8 %collective-permute-start.12 = (bf16[168,1152]{1,0:T(8,128)(2,1)S(1)}, bf16[168,1152]{1,0:T(8,128)(2,1)S(1)}, u32[]{:S(2)}, u32[]{:S(2)}) collective-permute-start(bf16[168,1152]{1,0:T(8,128)(2,1)S(1)} %collective-permute-done.10.rest_7_), channel_id=1, source_target_pairs={{0,2},{1,3},{2,0},{3,1},{4,6},{5,7},{6,4},{7,5},{8,10},{9,11},{10,... | collective-permute-start | bytes 1161224 | tf_op jit(solution)/shard_map/ppermute | solution.py:107
  36.7 3.7 %collective-permute-start.9 = (bf16[160,1152]{1,0:T(8,128)(2,1)S(1)}, bf16[160,1152]{1,0:T(8,128)(2,1)S(1)}, u32[]{:S(2)}, u32[]{:S(2)}) collective-permute-start(bf16[160,1152]{1,0:T(8,128)(2,1)S(1)} %collective-permute-done.8.rest_4_), channel_id=1, source_target_pairs={{0,2},{1,3},{2,0},{3,1},{4,6},{5,7},{6,4},{7,5},{8,10},{9,11},{10,... | collective-permute-start | bytes 1105928 | tf_op jit(solution)/shard_map/ppermute | solution.py:107

commit v4 on v3

--- a/solution.py
+++ b/solution.py
@@ -212,8 +212,8 @@
     group, side = lax.axis_index("dp"), lax.axis_index("fsdp")
 
     count = total // 4
-    for sources, target in ((texts, text), (images, zi)):
-        for k, source in enumerate(sources):
+    for sources, target, skip in ((texts, text, 1), (images, zi, 0)):
+        for k, source in enumerate(sources[skip:], skip):
             target[pl.ds(k * count, count)] = source[:count]
     match = pair_indices(rows, total, images, side)
     late = pl.ds(half, half)

time: 49.4 us -> 49.4 us (level)
  no operation moved by 1% of the time
where the time goes in v4:
time: 49.4 us; the launch traced here: 49.1 us
  waiting for transfers between devices  19.4 us (39%)
  Pallas kernels  12.3 us (25%)
  starting transfers between devices  11.6 us (23%)
  local copies, waits for them, and re-layouts  3.42 us (7%)
  between operations  2.08 us (4%)
    ppermute x13, waiting for transfers between devices, across(): lax.ppermute(block, ('dp', 'fsdp'), [(i, i ^ bits) for i in range(count)])  19.4 us
    ppermute x13, starting transfers between devices, across(): lax.ppermute(block, ('dp', 'fsdp'), [(i, i ^ bits) for i in range(count)])  11.6 us
    pallas_call x1, Pallas kernels, gathered_plan(): pl.pallas_call(batch_kernel, out_shape=(jax.ShapeDtypeStruct((rows, width...  8.57 us
    pallas_call x1, Pallas kernels, gathered_plan(): pl.pallas_call(early_kernel, out_shape=(jax.ShapeDtypeStruct((total // 2,...  2.14 us
    pallas_call x1, Pallas kernels, gathered_plan(): pl.pallas_call(own_kernel, out_shape=(jax.ShapeDtypeStruct((2, rows + 4,...  1.63 us
    dynamic_slice x1, local copies, waits for them, and re-layouts, gathered_plan(): quarter = lax.dynamic_slice_in_dim(matrix, core * half, half, 0)  1.15 us
  transfers between devices with their start and end apart: 13, of which 7 were waited for; matrix products, arithmetic and copies ran while one was open for 6% of the time, Pallas kernels for 4%

profile of v4, /device:TPU:0, one launch (start us, length us, event | category | flops | bytes accessed | tf_op | source)
XLA Modules:
  0.0 49.1 jit_solution(11526589133857184839)
XLA Ops:
  0.6 1.6 %own_block.1 = (bf16[2,24,1152]{2,1,0:T(8,128)(2,1)}, bf16[40,1152]{1,0:T(8,128)(2,1)}) custom-call(bf16[20,1152]{1,0:T(8,128)(2,1)} %image.3, bf16[20,1152]{1,0:T(8,128)(2,1)} %text.1, s32[1,40]{1,0:T(1,128)} %bitcast.11), custom_call_target="tpu_custom_call" | custom-call | tf_op jit(solution)/shard_map/own_block/pallas_call | solution.py:278
  2.3 5.0 %collective-permute-start.2 = (bf16[40,1152]{1,0:T(8,128)(2,1)}, bf16[40,1152]{1,0:T(8,128)(2,1)S(1)}, u32[]{:S(2)}, u32[]{:S(2)}) collective-permute-start(bf16[40,1152]{1,0:T(8,128)(2,1)} %get-tuple-element.18), channel_id=1, source_target_pairs={{0,17},{1,16},{2,19},{3,18},{4,21},{5,20},{6,23},{7,22},{8,25},{9,... | collective-permute-start | bytes 276488 | tf_op jit(solution)/shard_map/ppermute | solution.py:107
  7.3 0.5 %collective-permute-start = (bf16[40,1152]{1,0:T(8,128)(2,1)}, bf16[40,1152]{1,0:T(8,128)(2,1)S(1)}, u32[]{:S(2)}, u32[]{:S(2)}) collective-permute-start(bf16[40,1152]{1,0:T(8,128)(2,1)} %get-tuple-element.18), channel_id=1, source_target_pairs={{0,1},{1,0},{2,3},{3,2},{4,5},{5,4},{6,7},{7,6},{8,9},{9,8},{10,11... | collective-permute-start | bytes 276488 | tf_op jit(solution)/shard_map/ppermute | solution.py:107
  7.8 0.1 collective-permute-start.1
  7.8 0.8 %slice_bitcast_fusion.3 = bf16[2,1152]{1,0:T(2,128)(2,1)S(1)} fusion(bf16[2,24,1152]{2,1,0:T(8,128)(2,1)} %get-tuple-element.19), kind=kLoop, calls=%fused_computation.6 | loop fusion | bytes 9216 | tf_op jit(solution)/shard_map/squeeze | solution.py:299
  8.6 0.9 %fusion.2 = (bf16[20,1152]{1,0:T(8,128)(2,1)S(1)}, bf16[20,1152]{1,0:T(8,128)(2,1)S(1)}) fusion(bf16[40,1152]{1,0:T(8,128)(2,1)} %get-tuple-element.18), kind=kLoop, calls=%fused_computation.11 | loop fusion | bytes 184320 | tf_op jit(solution)/shard_map/slice | solution.py:301
  10.8 1.1 %constant_dynamic-slice_fusion = bf16[288,1152]{1,0:T(8,128)(2,1)S(1)} fusion(bf16[576,1152]{1,0:T(8,128)(2,1)} %matrix_own.1, s32[]{:T(128)S(6)} %select_n.11), kind=kLoop, calls=%fused_computation.8 | loop fusion | bytes 1327108 | tf_op jit(solution)/shard_map/dynamic_slice | solution.py:298
  12.0 0.1 maximum_bitcast_fusion.scalars
  12.0 0.4 collective-permute-done.2
  12.5 0.4 collective-permute-done
  12.9 4.1 %collective-permute-done.1 = bf16[2,24,1152]{2,1,0:T(8,128)(2,1)S(1)} collective-permute-done((bf16[2,24,1152]{2,1,0:T(8,128)(2,1)}, bf16[2,24,1152]{2,1,0:T(8,128)(2,1)S(1)}, u32[]{:S(2)}, u32[]{:S(2)}) %collective-permute-start.1) | collective-permute-done | bytes 110624 | tf_op jit(solution)/shard_map/ppermute | solution.py:107
  17.0 0.0 copy-start
  17.0 0.5 concatenate.16
  17.5 0.8 %collective-permute-start.4 = (bf16[80,1152]{1,0:T(8,128)(2,1)S(1)}, bf16[80,1152]{1,0:T(8,128)(2,1)S(1)}, u32[]{:S(2)}, u32[]{:S(2)}) collective-permute-start(bf16[80,1152]{1,0:T(8,128)(2,1)S(1)} %pad_maximum_fusion.2), channel_id=1, source_target_pairs={{0,8},{1,9},{2,10},{3,11},{4,12},{5,13},{6,14},{7,15},{8,0},{9,1},... | collective-permute-start | bytes 552968 | tf_op jit(solution)/shard_map/ppermute | solution.py:107
  18.4 1.6 %collective-permute-start.5 = (bf16[88,1152]{1,0:T(8,128)(2,1)S(1)}, bf16[88,1152]{1,0:T(8,128)(2,1)S(1)}, u32[]{:S(2)}, u32[]{:S(2)}) collective-permute-start(bf16[88,1152]{1,0:T(8,128)(2,1)S(1)} %concatenate.16), channel_id=1, source_target_pairs={{0,4},{1,5},{2,6},{3,7},{4,0},{5,1},{6,2},{7,3},{8,12},{9,13},{10,... | collective-permute-start | bytes 608264 | tf_op jit(solution)/shard_map/ppermute | solution.py:107
  19.9 0.5 %collective-permute-start.3 = (bf16[288,1152]{1,0:T(8,128)(2,1)S(1)}, bf16[288,1152]{1,0:T(8,128)(2,1)S(1)}, u32[]{:S(2)}, u32[]{:S(2)}) collective-permute-start(bf16[288,1152]{1,0:T(8,128)(2,1)S(1)} %constant_dynamic-slice_fusion), channel_id=1, source_target_pairs={{0,1},{1,0},{2,3},{3,2},{4,5},{5,4},{6,7},{7,6},{8,9},{9,8},{10,11... | collective-permute-start | bytes 1990664 | tf_op jit(solution)/shard_map/ppermute | solution.py:107
  20.4 3.0 %collective-permute-done.4 = bf16[80,1152]{1,0:T(8,128)(2,1)S(1)} collective-permute-done((bf16[80,1152]{1,0:T(8,128)(2,1)S(1)}, bf16[80,1152]{1,0:T(8,128)(2,1)S(1)}, u32[]{:S(2)}, u32[]{:S(2)}) %collective-permute-start.4) | collective-permute-done | bytes 184352 | tf_op jit(solution)/shard_map/ppermute | solution.py:107
  23.4 1.7 %collective-permute-done.5 = bf16[88,1152]{1,0:T(8,128)(2,1)S(1)} collective-permute-done((bf16[88,1152]{1,0:T(8,128)(2,1)S(1)}, bf16[88,1152]{1,0:T(8,128)(2,1)S(1)}, u32[]{:S(2)}, u32[]{:S(2)}) %collective-permute-start.5) | collective-permute-done | bytes 202784 | tf_op jit(solution)/shard_map/ppermute | solution.py:107
  25.2 0.0 copy-start.1
  25.2 0.1 collective-permute-start.6
  25.3 0.6 %collective-permute-start.10 = (bf16[168,1152]{1,0:T(8,128)(2,1)S(1)}, bf16[168,1152]{1,0:T(8,128)(2,1)S(1)}, u32[]{:S(2)}, u32[]{:S(2)}) collective-permute-start(bf16[168,1152]{1,0:T(8,128)(2,1)S(1)} %pad_maximum_fusion.rest_6_), channel_id=1, source_target_pairs={{0,8},{1,9},{2,10},{3,11},{4,12},{5,13},{6,14},{7,15},{8,0},{9,1},... | collective-permute-start | bytes 1161224 | tf_op jit(solution)/shard_map/ppermute | solution.py:107
  25.9 1.5 %collective-permute-start.8 = (bf16[160,1152]{1,0:T(8,128)(2,1)S(1)}, bf16[160,1152]{1,0:T(8,128)(2,1)S(1)}, u32[]{:S(2)}, u32[]{:S(2)}) collective-permute-start(bf16[160,1152]{1,0:T(8,128)(2,1)S(1)} %pad_maximum_fusion.1.rest_0_.rest_2_), channel_id=1, source_target_pairs={{0,4},{1,5},{2,6},{3,7},{4,0},{5,1},{6,2},{7,3},{8,12},{9,13},{10,... | collective-permute-start | bytes 1105928 | tf_op jit(solution)/shard_map/ppermute | solution.py:107
  27.3 0.0 collective-permute-done.6.rest_1_.rest_3_
  27.3 8.8 %collective-permute-done.3.matrix_near = bf16[288,1152]{1,0:T(8,128)(2,1)S(1)} collective-permute-done((bf16[288,1152]{1,0:T(8,128)(2,1)S(1)}, bf16[288,1152]{1,0:T(8,128)(2,1)S(1)}, u32[]{:S(2)}, u32[]{:S(2)}) %collective-permute-start.3) | collective-permute-done | bytes 663584 | tf_op jit(solution)/shard_map/ppermute | solution.py:107
  36.2 0.0 collective-permute-start.7
  36.2 0.5 %collective-permute-start.11 = (bf16[168,1152]{1,0:T(8,128)(2,1)S(1)}, bf16[168,1152]{1,0:T(8,128)(2,1)S(1)}, u32[]{:S(2)}, u32[]{:S(2)}) collective-permute-start(bf16[168,1152]{1,0:T(8,128)(2,1)S(1)} %pad_maximum_fusion.rest_6_), channel_id=1, source_target_pairs={{0,2},{1,3},{2,0},{3,1},{4,6},{5,7},{6,4},{7,5},{8,10},{9,11},{10,... | collective-permute-start | bytes 1161224 | tf_op jit(solution)/shard_map/ppermute | solution.py:107
  36.7 0.0 collective-permute-done.10.rest_7_
  36.7 0.0 collective-permute-start.12
  36.7 0.0 collective-permute-done.8.rest_4_
  36.7 0.5 %collective-permute-start.9 = (bf16[160,1152]{1,0:T(8,128)(2,1)S(1)}, bf16[160,1152]{1,0:T(8,128)(2,1)S(1)}, u32[]{:S(2)}, u32[]{:S(2)}) collective-permute-start(bf16[160,1152]{1,0:T(8,128)(2,1)S(1)} %collective-permute-done.8.rest_4_), channel_id=1, source_target_pairs={{0,2},{1,3},{2,0},{3,1},{4,6},{5,7},{6,4},{7,5},{8,10},{9,11},{10,... | collective-permute-start | bytes 1105928 | tf_op jit(solution)/shard_map/ppermute | solution.py:107
  37.2 1.1 %collective-permute-done.7.matrix_far = bf16[288,1152]{1,0:T(8,128)(2,1)S(1)} collective-permute-done((bf16[288,1152]{1,0:T(8,128)(2,1)S(1)}, bf16[288,1152]{1,0:T(8,128)(2,1)S(1)}, u32[]{:S(2)}, u32[]{:S(2)}) %collective-permute-start.7) | collective-permute-done | bytes 663584 | tf_op jit(solution)/shard_map/ppermute | solution.py:107
  38.3 0.0 copy-done
  38.3 2.1 %early_texts.1 = (bf16[320,1152]{1,0:T(8,128)(2,1)S(1)}, f32[320,1152]{1,0:T(8,128)S(1)}, bf16[576,256]{1,0:T(8,128)(2,1)S(1)}, bf16[1152,1152]{1,0:T(8,128)(2,1)S(1)}) custom-call(bf16[576,1152]{1,0:T(8,128)(2,1)S(1)} %copy-done, bf16[288,1152]{1,0:T(8,128)(2,1)S(1)} %collective-permute-done.3.matrix_near, ...), custom_call_target="tpu_custom_call" | custom-call | tf_op jit(solution)/shard_map/early_texts/pallas_call | solution.py:319
  40.4 0.0 collective-permute-done.11.rest_8_
  40.5 0.0 collective-permute-done.9.rest_5_
  40.5 0.0 collective-permute-done.12.rest_9_
  40.5 0.0 copy-done.1
  40.5 8.6 %batch.1 = (f32[20,1152]{1,0:T(8,128)}, f32[20,1152]{1,0:T(8,128)}, f32[576,1152]{1,0:T(8,128)}) custom-call(f32[1,2]{1,0:T(1,128)S(1)} %maximum_bitcast_fusion.scalars, bf16[20,1152]{1,0:T(8,128)(2,1)S(1)} %copy-done.1, bf16[320,1152]{1,0:T(8,128)(2,1)S(1)} %get-tuple-element.28.zt_early, f32[320,1152]{1,0:T(8,128)S(1)} %get-tuple-element.29.projected_early, ...), custom_call_target="tpu_custom_call" | custom-call | tf_op jit(solution)/shard_map/batch/pallas_call | solution.py:335
  (12 shorter events, 0.2 us)
Async XLA Ops:
  2.3 10.2 %collective-permute-start.2 = (bf16[40,1152]{1,0:T(8,128)(2,1)}, bf16[40,1152]{1,0:T(8,128)(2,1)S(1)}, u32[]{:S(2)}, u32[]{:S(2)}) collective-permute-start(bf16[40,1152]{1,0:T(8,128)(2,1)} %get-tuple-element.18), channel_id=1, source_target_pairs={{0,17},{1,16},{2,19},{3,18},{4,21},{5,20},{6,23},{7,22},{8,25},{9,... | collective-permute-start | bytes 276488 | tf_op jit(solution)/shard_map/ppermute | solution.py:107
  7.3 5.6 %collective-permute-start = (bf16[40,1152]{1,0:T(8,128)(2,1)}, bf16[40,1152]{1,0:T(8,128)(2,1)S(1)}, u32[]{:S(2)}, u32[]{:S(2)}) collective-permute-start(bf16[40,1152]{1,0:T(8,128)(2,1)} %get-tuple-element.18), channel_id=1, source_target_pairs={{0,1},{1,0},{2,3},{3,2},{4,5},{5,4},{6,7},{7,6},{8,9},{9,8},{10,11... | collective-permute-start | bytes 276488 | tf_op jit(solution)/shard_map/ppermute | solution.py:107
  7.8 9.2 %collective-permute-start.1 = (bf16[2,24,1152]{2,1,0:T(8,128)(2,1)}, bf16[2,24,1152]{2,1,0:T(8,128)(2,1)S(1)}, u32[]{:S(2)}, u32[]{:S(2)}) collective-permute-start(bf16[2,24,1152]{2,1,0:T(8,128)(2,1)} %get-tuple-element.19), channel_id=1, source_target_pairs={{0,16},{1,17},{2,18},{3,19},{4,20},{5,21},{6,22},{7,23},{8,24},{9,... | collective-permute-start | bytes 331784 | tf_op jit(solution)/shard_map/ppermute | solution.py:107
  17.0 21.3 %copy-start = (bf16[576,1152]{1,0:T(8,128)(2,1)S(1)}, bf16[576,1152]{1,0:T(8,128)(2,1)}, u32[]{:S(2)}) copy-start(bf16[576,1152]{1,0:T(8,128)(2,1)} %matrix_own.1) | copy-start | bytes 3981316
  17.5 5.9 %collective-permute-start.4 = (bf16[80,1152]{1,0:T(8,128)(2,1)S(1)}, bf16[80,1152]{1,0:T(8,128)(2,1)S(1)}, u32[]{:S(2)}, u32[]{:S(2)}) collective-permute-start(bf16[80,1152]{1,0:T(8,128)(2,1)S(1)} %pad_maximum_fusion.2), channel_id=1, source_target_pairs={{0,8},{1,9},{2,10},{3,11},{4,12},{5,13},{6,14},{7,15},{8,0},{9,1},... | collective-permute-start | bytes 552968 | tf_op jit(solution)/shard_map/ppermute | solution.py:107
  18.4 6.7 %collective-permute-start.5 = (bf16[88,1152]{1,0:T(8,128)(2,1)S(1)}, bf16[88,1152]{1,0:T(8,128)(2,1)S(1)}, u32[]{:S(2)}, u32[]{:S(2)}) collective-permute-start(bf16[88,1152]{1,0:T(8,128)(2,1)S(1)} %concatenate.16), channel_id=1, source_target_pairs={{0,4},{1,5},{2,6},{3,7},{4,0},{5,1},{6,2},{7,3},{8,12},{9,13},{10,... | collective-permute-start | bytes 608264 | tf_op jit(solution)/shard_map/ppermute | solution.py:107
  19.9 16.3 %collective-permute-start.3 = (bf16[288,1152]{1,0:T(8,128)(2,1)S(1)}, bf16[288,1152]{1,0:T(8,128)(2,1)S(1)}, u32[]{:S(2)}, u32[]{:S(2)}) collective-permute-start(bf16[288,1152]{1,0:T(8,128)(2,1)S(1)} %constant_dynamic-slice_fusion), channel_id=1, source_target_pairs={{0,1},{1,0},{2,3},{3,2},{4,5},{5,4},{6,7},{7,6},{8,9},{9,8},{10,11... | collective-permute-start | bytes 1990664 | tf_op jit(solution)/shard_map/ppermute | solution.py:107
  25.2 15.3 %copy-start.1 = (bf16[20,1152]{1,0:T(8,128)(2,1)S(1)}, bf16[20,1152]{1,0:T(8,128)(2,1)}, u32[]{:S(2)}) copy-start(bf16[20,1152]{1,0:T(8,128)(2,1)} %image.3) | copy-start | bytes 138244
  25.2 2.2 %collective-permute-start.6 = (bf16[160,1152]{1,0:T(8,128)(2,1)S(1)}, bf16[160,1152]{1,0:T(8,128)(2,1)S(1)}, u32[]{:S(2)}, u32[]{:S(2)}) collective-permute-start(bf16[160,1152]{1,0:T(8,128)(2,1)S(1)} %pad_maximum_fusion.1.rest_0_.rest_2_), channel_id=1, source_target_pairs={{0,2},{1,3},{2,0},{3,1},{4,6},{5,7},{6,4},{7,5},{8,10},{9,11},{10,... | collective-permute-start | bytes 1105928 | tf_op jit(solution)/shard_map/ppermute | solution.py:107
  25.3 11.4 %collective-permute-start.10 = (bf16[168,1152]{1,0:T(8,128)(2,1)S(1)}, bf16[168,1152]{1,0:T(8,128)(2,1)S(1)}, u32[]{:S(2)}, u32[]{:S(2)}) collective-permute-start(bf16[168,1152]{1,0:T(8,128)(2,1)S(1)} %pad_maximum_fusion.rest_6_), channel_id=1, source_target_pairs={{0,8},{1,9},{2,10},{3,11},{4,12},{5,13},{6,14},{7,15},{8,0},{9,1},... | collective-permute-start | bytes 1161224 | tf_op jit(solution)/shard_map/ppermute | solution.py:107
  25.9 10.9 %collective-permute-start.8 = (bf16[160,1152]{1,0:T(8,128)(2,1)S(1)}, bf16[160,1152]{1,0:T(8,128)(2,1)S(1)}, u32[]{:S(2)}, u32[]{:S(2)}) collective-permute-start(bf16[160,1152]{1,0:T(8,128)(2,1)S(1)} %pad_maximum_fusion.1.rest_0_.rest_2_), channel_id=1, source_target_pairs={{0,4},{1,5},{2,6},{3,7},{4,0},{5,1},{6,2},{7,3},{8,12},{9,13},{10,... | collective-permute-start | bytes 1105928 | tf_op jit(solution)/shard_map/ppermute | solution.py:107
  36.2 2.1 %collective-permute-start.7 = (bf16[288,1152]{1,0:T(8,128)(2,1)S(1)}, bf16[288,1152]{1,0:T(8,128)(2,1)S(1)}, u32[]{:S(2)}, u32[]{:S(2)}) collective-permute-start(bf16[288,1152]{1,0:T(8,128)(2,1)S(1)} %collective-permute-done.3.matrix_near), channel_id=1, source_target_pairs={{0,2},{1,3},{2,0},{3,1},{4,6},{5,7},{6,4},{7,5},{8,10},{9,11},{10,... | collective-permute-start | bytes 1990664 | tf_op jit(solution)/shard_map/ppermute | solution.py:107
  36.2 4.3 %collective-permute-start.11 = (bf16[168,1152]{1,0:T(8,128)(2,1)S(1)}, bf16[168,1152]{1,0:T(8,128)(2,1)S(1)}, u32[]{:S(2)}, u32[]{:S(2)}) collective-permute-start(bf16[168,1152]{1,0:T(8,128)(2,1)S(1)} %pad_maximum_fusion.rest_6_), channel_id=1, source_target_pairs={{0,2},{1,3},{2,0},{3,1},{4,6},{5,7},{6,4},{7,5},{8,10},{9,11},{10,... | collective-permute-start | bytes 1161224 | tf_op jit(solution)/shard_map/ppermute | solution.py:107
  36.7 3.8 %collective-permute-start.12 = (bf16[168,1152]{1,0:T(8,128)(2,1)S(1)}, bf16[168,1152]{1,0:T(8,128)(2,1)S(1)}, u32[]{:S(2)}, u32[]{:S(2)}) collective-permute-start(bf16[168,1152]{1,0:T(8,128)(2,1)S(1)} %collective-permute-done.10.rest_7_), channel_id=1, source_target_pairs={{0,2},{1,3},{2,0},{3,1},{4,6},{5,7},{6,4},{7,5},{8,10},{9,11},{10,... | collective-permute-start | bytes 1161224 | tf_op jit(solution)/shard_map/ppermute | solution.py:107
  36.7 3.7 %collective-permute-start.9 = (bf16[160,1152]{1,0:T(8,128)(2,1)S(1)}, bf16[160,1152]{1,0:T(8,128)(2,1)S(1)}, u32[]{:S(2)}, u32[]{:S(2)}) collective-permute-start(bf16[160,1152]{1,0:T(8,128)(2,1)S(1)} %collective-permute-done.8.rest_4_), channel_id=1, source_target_pairs={{0,2},{1,3},{2,0},{3,1},{4,6},{5,7},{6,4},{7,5},{8,10},{9,11},{10,... | collective-permute-start | bytes 1105928 | tf_op jit(solution)/shard_map/ppermute | solution.py:107
